TPU v7x, 256 devices: a whole 4x4x8 slice. The times are simulated.
256 devices in a mesh: depth: 4 (over y), lat: 64 (over x, z, core).
Axes of the slice: x: 4, y: 4, z: 8, core: 2. Of those that a mesh axis runs over, the one named last changes fastest.
Arguments:
- diag_blocks: float32 [4, 256, 128, 128], P('depth', 'lat'), as said below
- coupling: float32 [4, 256, 8, 128, 128], P('depth', 'lat'), may hold values from -0.2 to 0.2
- offsets: int32 [4, 256, 8], P('depth', 'lat'), may hold values from -8 to 7, as said below
- arrow_blocks: float32 [4, 256, 4, 128, 128], P('depth', 'lat'), may hold values from -0.9 to 0.9
- arrow_index: int32 [4, 256, 4], P('depth', 'lat'), may hold values from 0 to 7, all different within a row
- tip: float32 [1024, 1024], replicated, may hold values from -6 to 6
Outputs:
- factor: float32 [4, 256, 128, 128], P('depth', 'lat')
- handed: float32 [4, 256, 128, 128], P('depth', 'lat')
- schur_tip: float32 [1024, 1024], replicated
Inputs may be any that keep to these rules, and one draw needn't show every extreme that they name: The 8 offsets of one block row are different. `arrow_index`: the 4 indices of one block row are different. `diag_blocks`: each block is symmetric positive definite.
All inputs are finite; a program needn't handle non-finite values.
Results may differ from a plain program's by a relative error of at most 0.0003.
Values sent between devices are 32-bit elements; how exact they have to be, the bound alone decides.
A program may use at most 128 MiB of HBM per device.

v0:
```python
import jax
import jax.numpy as jnp
from jax import lax
from jax.sharding import PartitionSpec as P

REACH = 8
MB = 8


HIGH = lax.Precision.HIGHEST


def from_behind(value, axis, steps):
    count = lax.axis_size(axis)
    initial, last = (max(0, -steps), min(count, count - steps))
    return lax.ppermute(value, axis, [(source, source + steps) for source in range(initial, last)])


def factor_one(matrix):
    lower_factor = jnp.linalg.cholesky(matrix)
    identity = jnp.eye(matrix.shape[0], dtype=matrix.dtype)
    inverse = jax.scipy.linalg.cho_solve((lower_factor, True), identity)
    return (lower_factor, inverse)


def factorize(blocks):
    return jax.vmap(factor_one)(blocks)


def schur_update(chosen, coupling):
    inner = jnp.einsum("nwbc,nwcd->nwbd", chosen, coupling, precision=HIGH)
    return -jnp.einsum("nwba,nwbd->nad", coupling, inner, precision=HIGH)


def arrow_term(inverse, blocks, index, arrow_count):
    block_size = blocks.shape[-1]
    placing = (index[:, :, None] == jnp.arange(arrow_count, dtype=jnp.int32)[None, None, :]).astype(
        jnp.float32
    )
    carried = jnp.einsum("nab,nsbc->nsac", inverse, blocks, precision=HIGH)
    inner = jnp.einsum("nsba,ntbc->nsatc", blocks, carried, precision=HIGH)
    placed = jnp.einsum("ntq,nsatc->nsaqc", placing, inner, precision=HIGH)
    total = jnp.einsum("nsm,nsaqc->maqc", placing, placed, precision=HIGH)
    return total.reshape(arrow_count * block_size, arrow_count * block_size)


def window_panels(inverse):
    block_count = inverse.shape[0]
    reach_devices = (REACH + block_count - 1) // block_count
    pieces = []
    for distance in range(-reach_devices, reach_devices + 1):
        if distance == 0:
            pieces.append(inverse)
        else:
            pieces.append(from_behind(inverse, "lat", -distance))
    return (jnp.concatenate(pieces, 0), reach_devices * block_count)


def select_panels(window, base_index, offsets):
    block_count, width = offsets.shape
    block_size = window.shape[-1]
    target = jnp.arange(block_count, dtype=jnp.int32)[:, None] + offsets + base_index
    selector = (
        target.reshape(-1)[:, None] == jnp.arange(window.shape[0], dtype=jnp.int32)[None, :]
    ).astype(jnp.float32)
    picked = jnp.dot(selector, window.reshape(window.shape[0], -1), precision=HIGH)
    return picked.reshape(block_count, width, block_size, block_size)


def body(diag_blocks, coupling, offsets, arrow_blocks, arrow_index, tip):
    layers = lax.axis_size("depth")
    my_layer = lax.axis_index("depth")
    own_blocks = diag_blocks[0]
    incoming = jnp.zeros_like(own_blocks)
    kept_lower = jnp.zeros_like(own_blocks)
    kept_inverse = jnp.zeros_like(own_blocks)
    kept_update = jnp.zeros_like(own_blocks)
    update = jnp.zeros_like(own_blocks)
    for layer_step in range(layers):
        if layer_step > 0:
            incoming = from_behind(update, "depth", 1)
        lower_factor, inverse = factorize(own_blocks + incoming)
        window, base_index = window_panels(inverse)
        update = schur_update(select_panels(window, base_index, offsets[0]), coupling[0])
        active = my_layer == layer_step
        kept_lower = jnp.where(active, lower_factor, kept_lower)
        kept_inverse = jnp.where(active, inverse, kept_inverse)
        kept_update = jnp.where(active, update, kept_update)
    term = arrow_term(kept_inverse, arrow_blocks[0], arrow_index[0], MB)
    schur_tip = tip - lax.psum(term, ("depth", "lat"))
    return (kept_lower[None], kept_update[None], schur_tip)


def solution(mesh):
    return jax.shard_map(
        body,
        mesh=mesh,
        in_specs=(
            P("depth", "lat", None, None),
            P("depth", "lat", None, None, None),
            P("depth", "lat", None),
            P("depth", "lat", None, None, None),
            P("depth", "lat", None),
            P(),
        ),
        out_specs=(P("depth", "lat", None, None), P("depth", "lat", None, None), P()),
        check_vma=False,
    )
```

profile of v0, /device:TPU:1, one launch (start us, length us, event | category | flops | bytes accessed | tf_op | source)
XLA Modules:
  0.0 799.6 jit_solution(10268709051617900299)
XLA Ops:
  7.3 1.2 copy.71
  8.5 1.0 fusion.82
  9.6 46.9 %custom-call.14 = f32[4,128,128]{2,1,0:T(8,128)S(1)} custom-call(f32[4,128,128]{2,1,0:T(8,128)S(1)} %copy.72), custom_call_target="Cholesky" | custom-call | tf_op jit(solution)/shard_map/vmap(jit(cholesky))/cholesky | solution.py:20
  56.8 39.3 %custom-call.15 = f32[4,1,128,128]{2,3,1,0:T(8,128)S(1)} custom-call(f32[4,1,128,128]{3,2,1,0:T(8,128)S(1)} %select_bitcast_fusion.3), custom_call_target="InvertDiagBlocksLowerTriangular" | custom-call | tf_op jit(solution)/shard_map/vmap(jit(_cho_solve))/triangular_solve | solution.py:22
  97.1 4.4 collective-permute-start
  101.5 1.3 collective-permute-start.3
  102.8 2.9 collective-permute-start.2
  105.7 4.3 collective-permute-start.1
  110.1 3.1 collective-permute-done.1
  113.2 1.2 collective-permute-done.2
  114.6 2.0 fusion.31
  116.6 3.5 fusion.19
  120.1 3.5 fusion.43
  123.7 3.4 collective-permute-start.4
  127.1 4.2 collective-permute-done.4
  131.6 46.9 %custom-call.16 = f32[4,128,128]{2,1,0:T(8,128)S(1)} custom-call(f32[4,128,128]{2,1,0:T(8,128)S(1)} %copy.80), custom_call_target="Cholesky" | custom-call | tf_op jit(solution)/shard_map/vmap(jit(cholesky))/cholesky | solution.py:20
  178.8 39.3 %custom-call.17 = f32[4,1,128,128]{2,3,1,0:T(8,128)S(1)} custom-call(f32[4,1,128,128]{3,2,1,0:T(8,128)S(1)} %select_bitcast_fusion.2), custom_call_target="InvertDiagBlocksLowerTriangular" | custom-call | tf_op jit(solution)/shard_map/vmap(jit(_cho_solve))/triangular_solve | solution.py:22
  219.2 5.0 collective-permute-start.5
  224.2 3.5 collective-permute-start.6
  227.7 1.3 collective-permute-start.8
  229.0 2.2 collective-permute-start.7
  231.3 1.9 collective-permute-done.6
  233.2 7.0 collective-permute-done.7
  240.3 2.0 fusion.29
  242.3 3.5 fusion.15
  245.8 3.5 fusion.52
  249.4 4.3 collective-permute-start.9
  253.7 2.8 collective-permute-done.9
  256.8 46.9 %custom-call.18 = f32[4,128,128]{2,1,0:T(8,128)S(1)} custom-call(f32[4,128,128]{2,1,0:T(8,128)S(1)} %copy.88), custom_call_target="Cholesky" | custom-call | tf_op jit(solution)/shard_map/vmap(jit(cholesky))/cholesky | solution.py:20
  304.0 39.3 %custom-call.19 = f32[4,1,128,128]{2,3,1,0:T(8,128)S(1)} custom-call(f32[4,1,128,128]{3,2,1,0:T(8,128)S(1)} %select_bitcast_fusion.1), custom_call_target="InvertDiagBlocksLowerTriangular" | custom-call | tf_op jit(solution)/shard_map/vmap(jit(_cho_solve))/triangular_solve | solution.py:22
  344.4 5.1 collective-permute-start.10
  349.5 3.7 collective-permute-start.11
  353.3 1.3 collective-permute-start.13
  354.6 2.1 collective-permute-start.12
  356.9 9.2 %collective-permute-done.12 = f32[4,128,128]{2,1,0:T(8,128)S(1)} collective-permute-done((f32[4,128,128]{2,1,0:T(8,128)S(1)}, f32[4,128,128]{2,1,0:T(8,128)S(1)}, u32[]{:S(2)}, u32[]{:S(2)}) %collective-permute-start.12) | collective-permute-done | bytes 262176 | tf_op jit(solution)/shard_map/ppermute | solution.py:16
  366.3 2.0 fusion.27
  368.3 3.5 fusion.11
  371.8 3.5 fusion.61
  375.4 4.0 collective-permute-start.14
  379.4 3.6 collective-permute-done.14
  383.4 47.6 %custom-call.20 = f32[4,128,128]{2,1,0:T(8,128)} custom-call(f32[4,128,128]{2,1,0:T(8,128)S(1)} %copy.96), custom_call_target="Cholesky" | custom-call | tf_op jit(solution)/shard_map/vmap(jit(cholesky))/cholesky | solution.py:20
  430.9 1.1 select_reduce_fusion
  432.1 2.2 select_bitcast_fusion
  434.3 40.1 %custom-call.21 = f32[4,1,128,128]{2,3,1,0:T(8,128)S(1)} custom-call(f32[4,1,128,128]{3,2,1,0:T(8,128)} %get-tuple-element.5), custom_call_target="InvertDiagBlocksLowerTriangular" | custom-call | tf_op jit(solution)/shard_map/vmap(jit(_cho_solve))/triangular_solve | solution.py:22
  474.4 0.7 copy-done.14
  475.7 1.3 fusion.83
  477.1 2.0 convolution_bitcast_fusion.2
  479.1 5.0 convolution_bitcast_fusion.1
  484.1 5.3 copy.103
  489.4 6.6 convolution_bitcast_fusion
  496.0 12.1 %fusion.2 = f32[8,128,8,128]{3,0,2,1:T(8,128)S(1)} fusion(f32[4,4,128,8,128]{4,3,2,1,0:T(8,128)S(1)} %convolution_bitcast_fusion, s32[4,4]{1,0:T(4,128)S(1)} %bitcast.272), kind=kOutput, calls=%fused_computation.4 | convolution fusion | flops 201326720 | bytes 12582976 | tf_op jit(solution)/shard_map/nsm,nsaqc->maqc/dot_general | solution.py:43
  508.2 0.8 copy.105
  509.0 3.2 copy.169
  512.2 4.6 collective-permute-start.15
  516.8 3.3 collective-permute-start.16
  520.1 1.3 collective-permute-start.18
  521.4 1.9 collective-permute-start.17
  523.3 1.3 collective-permute-done.16
  524.7 9.2 %collective-permute-done.17 = f32[4,128,128]{2,1,0:T(8,128)S(1)} collective-permute-done((f32[4,128,128]{2,1,0:T(8,128)S(1)}, f32[4,128,128]{2,1,0:T(8,128)S(1)}, u32[]{:S(2)}, u32[]{:S(2)}) %collective-permute-start.17) | collective-permute-done | bytes 262176 | tf_op jit(solution)/shard_map/ppermute | solution.py:16
  534.1 2.0 fusion.25
  536.1 3.5 fusion.7
  539.7 4.2 fusion.76
  543.9 241.8 %all-reduce.2.cloned.1.call-done = f32[1024,1024]{1,0:T(8,128)} async-done(((f32[1024,1024]{1,0:T(8,128)}), f32[1024,1024]{1,0:T(8,128)}) %all-reduce.2.cloned.1.call-update) | async-done | bytes 4194320 | tf_op jit(solution)/shard_map/psum | solution.py:90
  785.8 6.8 sub.3
  (102 shorter events, 6.7 us)
Async XLA Ops:
  7.2 109.4 %copy-start = (f32[1,4,8,128,128]{4,3,2,1,0:T(8,128)S(1)}, f32[1,4,8,128,128]{4,3,2,1,0:T(8,128)}, u32[]{:S(2)}) copy-start(f32[1,4,8,128,128]{4,3,2,1,0:T(8,128)} %param.10) | copy-start | bytes 6291460
  7.2 778.6 %all-reduce.2.cloned.1.call-start = ((), (), s32[]{:S(2)}) async-start(), calls=%async_computation | async-start | bytes 8388608 | tf_op jit(solution)/shard_map/psum | solution.py:90
  8.5 101.6 %copy-start.16 = (s32[1,4,8]{2,1,0:T(4,128)S(1)}, s32[1,4,8]{2,1,0:T(4,128)}, u32[]{:S(2)}) copy-start(s32[1,4,8]{2,1,0:T(4,128)} %param.11) | copy-start | bytes 388
  97.1 17.3 %copy-start.5 = (f32[4,128,128]{2,1,0:T(8,128)}, f32[4,128,128]{2,1,0:T(8,128)S(1)}, u32[]{:S(2)}) copy-start(f32[4,128,128]{2,1,0:T(8,128)S(1)} %fusion.98) | copy-start | bytes 786436
  97.1 12.9 %collective-permute-start = (f32[4,128,128]{2,1,0:T(8,128)S(1)}, f32[4,128,128]{2,1,0:T(8,128)S(1)}, u32[]{:S(2)}, u32[]{:S(2)}) collective-permute-start(f32[4,128,128]{2,1,0:T(8,128)S(1)} %fusion.98), channel_id=1, source_target_pairs={{0,2},{1,3},{2,4},{3,5},{4,6},{5,7},{6,8},{7,9},{8,10},{9,11},{10,... | collective-permute-start | bytes 786440 | tf_op jit(solution)/shard_map/ppermute | solution.py:16
  101.5 12.9 %collective-permute-start.3 = (f32[4,128,128]{2,1,0:T(8,128)S(1)}, f32[4,128,128]{2,1,0:T(8,128)S(1)}, u32[]{:S(2)}, u32[]{:S(2)}) collective-permute-start(f32[4,128,128]{2,1,0:T(8,128)S(1)} %fusion.98), channel_id=1, source_target_pairs={{2,0},{3,1},{4,2},{5,3},{6,4},{7,5},{8,6},{9,7},{10,8},{11,9},{12,... | collective-permute-start | bytes 786440 | tf_op jit(solution)/shard_map/ppermute | solution.py:16
  102.8 11.6 %collective-permute-start.2 = (f32[4,128,128]{2,1,0:T(8,128)S(1)}, f32[4,128,128]{2,1,0:T(8,128)S(1)}, u32[]{:S(2)}, u32[]{:S(2)}) collective-permute-start(f32[4,128,128]{2,1,0:T(8,128)S(1)} %fusion.98), channel_id=1, source_target_pairs={{1,0},{2,1},{3,2},{4,3},{5,4},{6,5},{7,6},{8,7},{9,8},{10,9},{11,1... | collective-permute-start | bytes 786440 | tf_op jit(solution)/shard_map/ppermute | solution.py:16
  105.7 7.5 collective-permute-start.1
  120.1 11.2 %copy-start.1 = (f32[1,4,128,128]{3,2,1,0:T(8,128)S(1)}, f32[1,4,128,128]{3,2,1,0:T(8,128)}, u32[]{:S(2)}) copy-start(f32[1,4,128,128]{3,2,1,0:T(8,128)} %param.9) | copy-start | bytes 786436
  123.7 3.4 copy-start.8
  123.7 7.6 collective-permute-start.4
  178.5 54.6 %copy-start.3 = (f32[4,128,128]{2,1,0:T(8,128)}, f32[4,128,128]{2,1,0:T(8,128)S(1)}, u32[]{:S(2)}) copy-start(f32[4,128,128]{2,1,0:T(8,128)S(1)} %custom-call.16) | copy-start | bytes 786436
  219.2 21.2 %copy-start.6 = (f32[4,128,128]{2,1,0:T(8,128)}, f32[4,128,128]{2,1,0:T(8,128)S(1)}, u32[]{:S(2)}) copy-start(f32[4,128,128]{2,1,0:T(8,128)S(1)} %fusion.93) | copy-start | bytes 786436
  219.2 12.1 %collective-permute-start.5 = (f32[4,128,128]{2,1,0:T(8,128)S(1)}, f32[4,128,128]{2,1,0:T(8,128)S(1)}, u32[]{:S(2)}, u32[]{:S(2)}) collective-permute-start(f32[4,128,128]{2,1,0:T(8,128)S(1)} %fusion.93), channel_id=1, source_target_pairs={{0,2},{1,3},{2,4},{3,5},{4,6},{5,7},{6,8},{7,9},{8,10},{9,11},{10,... | collective-permute-start | bytes 786440 | tf_op jit(solution)/shard_map/ppermute | solution.py:16
  224.2 8.9 %collective-permute-start.6 = (f32[4,128,128]{2,1,0:T(8,128)S(1)}, f32[4,128,128]{2,1,0:T(8,128)S(1)}, u32[]{:S(2)}, u32[]{:S(2)}) collective-permute-start(f32[4,128,128]{2,1,0:T(8,128)S(1)} %fusion.93), channel_id=1, source_target_pairs={{0,1},{1,2},{2,3},{3,4},{4,5},{5,6},{6,7},{7,8},{8,9},{9,10},{10,1... | collective-permute-start | bytes 786440 | tf_op jit(solution)/shard_map/ppermute | solution.py:16
  227.7 12.4 %collective-permute-start.8 = (f32[4,128,128]{2,1,0:T(8,128)S(1)}, f32[4,128,128]{2,1,0:T(8,128)S(1)}, u32[]{:S(2)}, u32[]{:S(2)}) collective-permute-start(f32[4,128,128]{2,1,0:T(8,128)S(1)} %fusion.93), channel_id=1, source_target_pairs={{2,0},{3,1},{4,2},{5,3},{6,4},{7,5},{8,6},{9,7},{10,8},{11,9},{12,... | collective-permute-start | bytes 786440 | tf_op jit(solution)/shard_map/ppermute | solution.py:16
  229.0 11.1 %collective-permute-start.7 = (f32[4,128,128]{2,1,0:T(8,128)S(1)}, f32[4,128,128]{2,1,0:T(8,128)S(1)}, u32[]{:S(2)}, u32[]{:S(2)}) collective-permute-start(f32[4,128,128]{2,1,0:T(8,128)S(1)} %fusion.93), channel_id=1, source_target_pairs={{1,0},{2,1},{3,2},{4,3},{5,4},{6,5},{7,6},{8,7},{9,8},{10,9},{11,1... | collective-permute-start | bytes 786440 | tf_op jit(solution)/shard_map/ppermute | solution.py:16
  249.4 4.3 copy-start.10
  249.4 7.1 collective-permute-start.9
  303.7 53.1 %copy-start.4 = (f32[4,128,128]{2,1,0:T(8,128)}, f32[4,128,128]{2,1,0:T(8,128)S(1)}, u32[]{:S(2)}) copy-start(f32[4,128,128]{2,1,0:T(8,128)S(1)} %custom-call.18) | copy-start | bytes 786436
  344.3 22.0 %copy-start.7 = (f32[4,128,128]{2,1,0:T(8,128)}, f32[4,128,128]{2,1,0:T(8,128)S(1)}, u32[]{:S(2)}) copy-start(f32[4,128,128]{2,1,0:T(8,128)S(1)} %fusion.88) | copy-start | bytes 786436
  344.4 12.3 %collective-permute-start.10 = (f32[4,128,128]{2,1,0:T(8,128)S(1)}, f32[4,128,128]{2,1,0:T(8,128)S(1)}, u32[]{:S(2)}, u32[]{:S(2)}) collective-permute-start(f32[4,128,128]{2,1,0:T(8,128)S(1)} %fusion.88), channel_id=1, source_target_pairs={{0,2},{1,3},{2,4},{3,5},{4,6},{5,7},{6,8},{7,9},{8,10},{9,11},{10,... | collective-permute-start | bytes 786440 | tf_op jit(solution)/shard_map/ppermute | solution.py:16
  349.5 7.4 collective-permute-start.11
  353.3 12.9 %collective-permute-start.13 = (f32[4,128,128]{2,1,0:T(8,128)S(1)}, f32[4,128,128]{2,1,0:T(8,128)S(1)}, u32[]{:S(2)}, u32[]{:S(2)}) collective-permute-start(f32[4,128,128]{2,1,0:T(8,128)S(1)} %fusion.88), channel_id=1, source_target_pairs={{2,0},{3,1},{4,2},{5,3},{6,4},{7,5},{8,6},{9,7},{10,8},{11,9},{12,... | collective-permute-start | bytes 786440 | tf_op jit(solution)/shard_map/ppermute | solution.py:16
  354.6 11.6 %collective-permute-start.12 = (f32[4,128,128]{2,1,0:T(8,128)S(1)}, f32[4,128,128]{2,1,0:T(8,128)S(1)}, u32[]{:S(2)}, u32[]{:S(2)}) collective-permute-start(f32[4,128,128]{2,1,0:T(8,128)S(1)} %fusion.88), channel_id=1, source_target_pairs={{1,0},{2,1},{3,2},{4,3},{5,4},{6,5},{7,6},{8,7},{9,8},{10,9},{11,1... | collective-permute-start | bytes 786440 | tf_op jit(solution)/shard_map/ppermute | solution.py:16
  375.4 4.1 copy-start.12
  375.4 7.7 collective-permute-start.14
  430.9 46.1 %copy-start.2 = (f32[1,4,4,128,128]{4,3,2,1,0:T(8,128)S(1)}, f32[1,4,4,128,128]{4,3,2,1,0:T(8,128)}, u32[]{:S(2)}) copy-start(f32[1,4,4,128,128]{4,3,2,1,0:T(8,128)} %param.12) | copy-start | bytes 3145732
  474.4 0.7 copy-start.14
  484.1 5.3 copy-start.15
  512.2 11.1 %collective-permute-start.15 = (f32[4,128,128]{2,1,0:T(8,128)S(1)}, f32[4,128,128]{2,1,0:T(8,128)S(1)}, u32[]{:S(2)}, u32[]{:S(2)}) collective-permute-start(f32[4,128,128]{2,1,0:T(8,128)S(1)} %fusion.83), channel_id=1, source_target_pairs={{0,2},{1,3},{2,4},{3,5},{4,6},{5,7},{6,8},{7,9},{8,10},{9,11},{10,... | collective-permute-start | bytes 786440 | tf_op jit(solution)/shard_map/ppermute | solution.py:16
  516.8 7.9 collective-permute-start.16
  520.1 13.9 %collective-permute-start.18 = (f32[4,128,128]{2,1,0:T(8,128)S(1)}, f32[4,128,128]{2,1,0:T(8,128)S(1)}, u32[]{:S(2)}, u32[]{:S(2)}) collective-permute-start(f32[4,128,128]{2,1,0:T(8,128)S(1)} %fusion.83), channel_id=1, source_target_pairs={{2,0},{3,1},{4,2},{5,3},{6,4},{7,5},{8,6},{9,7},{10,8},{11,9},{12,... | collective-permute-start | bytes 786440 | tf_op jit(solution)/shard_map/ppermute | solution.py:16
  521.4 12.6 %collective-permute-start.17 = (f32[4,128,128]{2,1,0:T(8,128)S(1)}, f32[4,128,128]{2,1,0:T(8,128)S(1)}, u32[]{:S(2)}, u32[]{:S(2)}) collective-permute-start(f32[4,128,128]{2,1,0:T(8,128)S(1)} %fusion.83), channel_id=1, source_target_pairs={{1,0},{2,1},{3,2},{4,3},{5,4},{6,5},{7,6},{8,7},{9,8},{10,9},{11,1... | collective-permute-start | bytes 786440 | tf_op jit(solution)/shard_map/ppermute | solution.py:16
  536.1 3.6 copy-start.9
  536.1 3.6 copy-start.11
  536.1 3.6 copy-start.13
Sparse Core Ops, SparseCore 0:
  512.3 273.3 all-reduce.1
where the time goes:
time: 807 us; the launch traced here: 800 us
  other arithmetic  359 us (44%)
  waiting for transfers between devices  286 us (35%)
  matrix products  67.4 us (8%)
  starting transfers between devices  60 us (7%)
  between operations  15.2 us (2%)
  local copies, waits for them, and re-layouts  13 us (2%)
    psum x1, waiting for transfers between devices, body(): schur_tip = tip - lax.psum(term, ('depth', 'lat'))  242 us
    another operation x13, other arithmetic, factor_one(): lower_factor = jnp.linalg.cholesky(matrix)  190 us
    another operation x8, other arithmetic, factor_one(): inverse = jax.scipy.linalg.cho_solve((lower_factor, True), identity)  161 us
    ppermute x19, starting transfers between devices, from_behind(): lax.ppermute(value, axis, [(source, source + steps) for source in range(i...  60 us
    ppermute x19, waiting for transfers between devices, from_behind(): lax.ppermute(value, axis, [(source, source + steps) for source in range(i...  43.7 us
  transfers between devices with their start and end apart: 20, of which 12 were waited for; matrix products, arithmetic and copies ran while one was open for 1% of the time, Pallas kernels for 0%

commit v1 on v0

v1 whole, which is shorter than its diff:
```python
import functools

import jax
import jax.numpy as jnp
from jax import lax
from jax.experimental import pallas as pl
from jax.experimental.pallas import tpu as pltpu
from jax.sharding import PartitionSpec as P

BS = 128
PANEL = 32
REACH = 8
MB = 8
F32 = jnp.float32
BF16 = jnp.bfloat16
VMEM = pl.BlockSpec(memory_space=pltpu.VMEM)
SMEM = pl.BlockSpec(memory_space=pltpu.SMEM)
MESH = pl.DeviceIdType.MESH
TILES = [(i, j) for i in range(MB) for j in range(i + 1)]
X, Z = 4, 8


def split2(x):
    high = x.astype(BF16)
    return high, (x - high.astype(F32)).astype(BF16)


def split3(x):
    high = x.astype(BF16)
    rest = x - high.astype(F32)
    middle = rest.astype(BF16)
    return high, middle, (rest - middle.astype(F32)).astype(BF16)


def dot(a, b):
    return jnp.dot(a, b, preferred_element_type=F32)


def dot_t(a, b):
    return lax.dot_general(a, b, (((0,), (0,)), ((), ())), preferred_element_type=F32)


def gram_exact(u, v):
    uh, um, ul = split3(u)
    vh, vm, vl = split3(v)
    return dot_t(
        jnp.concatenate([uh, uh, uh, um, um, ul], 0),
        jnp.concatenate([vh, vm, vl, vh, vm, vh], 0),
    )


def factor_kernel(a_ref, inc_ref, u_ref):
    count = a_ref.shape[0]
    lane = lax.broadcasted_iota(jnp.int32, (8, BS), 1)
    sub = lax.broadcasted_iota(jnp.int32, (8, BS), 0)
    groups = PANEL // 8
    spread = lambda x: jnp.broadcast_to(x, (8, BS))
    first = (lax.axis_index("depth") > 0).astype(F32)
    for m in range(count):
        u_ref[m] = jnp.where(first > 0, a_ref[m] + inc_ref[m], a_ref[m])
    for j0 in range(0, BS, PANEL):
        rows_of = [[u_ref[m, j0 + 8 * v : j0 + 8 * v + 8, :] for v in range(groups)] for m in range(count)]
        for g in range(groups):
            c0 = j0 + 8 * g
            for m in range(count):
                part = rows_of[m]
                cols = [[spread(part[v][:, c0 + k : c0 + k + 1]) for k in range(8)] for v in range(g, groups)]
                keep = (lane < c0) | (lane >= c0 + 8)
                x = jnp.where(keep, part[g], jnp.where(lane == c0 + sub, 1.0, 0.0))
                d = cols[0]
                scales, rows, low = [], [], {}
                for i in range(8):
                    scale = lax.rsqrt(spread(d[i][i : i + 1, :]))
                    li = d[i] * scale
                    for k in range(i + 1, 8):
                        low[k, i] = spread(li[k : k + 1, :])
                        d[k] = d[k] - li * low[k, i]
                    row = spread(x[i : i + 1, :]) * scale
                    scales.append(scale)
                    rows.append(row)
                    x = jnp.where(sub > i, x - li * row, jnp.where(sub == i, row, x))
                for k in range(1, 8):
                    for i in range(k):
                        x = jnp.where((sub == i) & (lane == c0 + k), low[k, i], x)
                part[g] = x
                for v in range(g + 1, groups):
                    d = cols[v - g]
                    x = jnp.where(keep, part[v], 0.0)
                    for i in range(8):
                        mi = d[i] * scales[i]
                        for k in range(i + 1, 8):
                            d[k] = d[k] - mi * low[k, i]
                        x = x - mi * rows[i]
                    part[v] = x
        for m in range(count):
            u = jnp.concatenate(rows_of[m], 0)
            u_ref[m, j0 : j0 + PANEL, :] = u
            end = j0 + PANEL
            if end < BS:
                ln = lax.broadcasted_iota(jnp.int32, u.shape, 1)
                sb = lax.broadcasted_iota(jnp.int32, u.shape, 0)
                full = gram_exact(u, jnp.where((ln < end) & (ln > j0 + sb), 0.0, u))
                rest = u_ref[m, end:, :]
                ln = lax.broadcasted_iota(jnp.int32, rest.shape, 1)
                rest = jnp.where((ln >= j0) & (ln < end), 0.0, rest)
                u_ref[m, end:, :] = rest - full[end:, :]


def factorize(blocks, incoming):
    return pl.pallas_call(
        factor_kernel,
        out_shape=jax.ShapeDtypeStruct(blocks.shape, F32),
        in_specs=[VMEM, VMEM],
        out_specs=VMEM,
    )(blocks, incoming)


def lower_part(u):
    row = lax.broadcasted_iota(jnp.int32, (BS, BS), 0)
    col = lax.broadcasted_iota(jnp.int32, (BS, BS), 1)
    return jnp.where(col <= row, u, 0.0)


def update_kernel(u_ref, c_ref, off_ref, handed_ref, inc_ref, window, wide, stacked, landed, lat_send, lat_recv, dep_send, dep_recv):
    depths, lats = lax.axis_size("depth"), lax.axis_size("lat")
    d, l = lax.axis_index("depth"), lax.axis_index("lat")
    count, width = off_ref.shape
    reach = REACH // count
    steps = [s for s in range(-reach, reach + 1) if s != 0]
    after, before = lax.rem(d + 1, depths), lax.rem(d + depths - 1, depths)

    barrier = pltpu.get_barrier_semaphore()
    for s in steps:
        pl.semaphore_signal(barrier, inc=1, device_id=(d, lax.rem(l + s + lats, lats)), device_id_type=MESH)
    pl.semaphore_signal(barrier, inc=1, device_id=(before, l), device_id_type=MESH)
    for m in range(count):
        window[REACH + m] = lower_part(u_ref[m])
    pl.semaphore_wait(barrier, len(steps) + 1)

    copies = []
    for at, s in enumerate(steps):
        copy = pltpu.make_async_remote_copy(
            src_ref=window.at[pl.ds(REACH, count)],
            dst_ref=window.at[pl.ds(REACH - s * count, count)],
            send_sem=lat_send.at[at],
            recv_sem=lat_recv.at[at],
            device_id=(d, lax.rem(l + s + lats, lats)),
            device_id_type=MESH,
        )
        copy.start()
        copies.append(copy)
    for copy in copies:
        copy.wait()
    for at in range(2 * REACH + count):
        distance = at // count - reach
        inside = (l + distance >= 0) & (l + distance < lats)
        high, low = split2(jnp.where(inside, window[at], 0.0))
        wide[at] = jnp.concatenate([high, low, high], 1)
    sends = []
    for m in range(count):
        for w in range(width):
            ch, cl = split2(c_ref[m, w])
            x = dot(wide[off_ref[m, w] + (m + REACH)], jnp.concatenate([ch, ch, cl], 0))
            xh, xl = split2(x)
            stacked[w * BS : (w + 1) * BS, :] = jnp.concatenate([xh, xl], 1)
        both = dot_t(stacked[:, :BS], stacked[...])
        cross = both[:, BS:]
        handed_ref[m] = -(both[:, :BS] + cross + cross.T)
        copy = pltpu.make_async_remote_copy(
            src_ref=handed_ref.at[m],
            dst_ref=landed.at[m],
            send_sem=dep_send.at[m],
            recv_sem=dep_recv.at[m],
            device_id=(after, l),
            device_id_type=MESH,
        )
        copy.start()
        sends.append(copy)
    for copy in sends:
        copy.wait()
    inc_ref[...] = landed[...]


def exchange(u, coupling, offsets, step):
    count, width = offsets.shape
    shape = jax.ShapeDtypeStruct((count, BS, BS), F32)
    neighbours = 2 * (REACH // count)
    return pl.pallas_call(
        update_kernel,
        out_shape=(shape, shape),
        in_specs=[VMEM, VMEM, SMEM],
        out_specs=(VMEM, VMEM),
        scratch_shapes=[
            pltpu.VMEM((2 * REACH + count, BS, BS), F32),
            pltpu.VMEM((2 * REACH + count, BS, 3 * BS), BF16),
            pltpu.VMEM((width * BS, 2 * BS), BF16),
            pltpu.VMEM((count, BS, BS), F32),
            pltpu.SemaphoreType.DMA((neighbours,)),
            pltpu.SemaphoreType.DMA((neighbours,)),
            pltpu.SemaphoreType.DMA((count,)),
            pltpu.SemaphoreType.DMA((count,)),
        ],
        compiler_params=pltpu.CompilerParams(
            collective_id=step, has_side_effects=True, vmem_limit_bytes=40 * 1024 * 1024
        ),
    )(u, coupling, offsets)


def arrow_kernel(u_ref, b_ref, idx_ref, g_ref, l_ref, left, right):
    count, width = idx_ref.shape
    row = lax.broadcasted_iota(jnp.int32, (BS, BS), 0)
    col = lax.broadcasted_iota(jnp.int32, (BS, BS), 1)
    g_ref[...] = jnp.zeros_like(g_ref)
    for n in range(count):
        u = u_ref[n]
        l_ref[n] = jnp.where(col > row, u, jnp.where(col == row, 1.0 / u, 0.0)).T
        high, low = split2(jnp.where(col <= row, u, 0.0))
        lhs = jnp.concatenate([high, low, high], 1)
        ranks = []
        for s in range(width):
            rank = 0
            for t in range(width):
                if t != s:
                    rank = rank + (idx_ref[n, t] < idx_ref[n, s]).astype(jnp.int32)
            ranks.append(rank)
        for s in range(width):
            bh, bl = split2(b_ref[n, s])
            th, tl = split2(dot(lhs, jnp.concatenate([bh, bh, bl], 0)))
            at = pl.ds(pl.multiple_of(ranks[s] * BS, BS), BS)
            left[:, at] = jnp.concatenate([th, th, tl], 0)
            right[:, at] = jnp.concatenate([th, tl, th], 0)
        sorted_idx = [
            sum(jnp.where(ranks[s] == a, idx_ref[n, s], 0) for s in range(width)) for a in range(width)
        ]
        for a in range(width):
            products = dot_t(left[:, a * BS : (a + 1) * BS], right[:, : (a + 1) * BS])
            for b in range(a + 1):
                i, j = sorted_idx[a], sorted_idx[b]
                g_ref[i * (i + 1) // 2 + j] += products[:, b * BS : (b + 1) * BS]


def arrow_terms(u, blocks, index):
    count, width = index.shape
    return pl.pallas_call(
        arrow_kernel,
        out_shape=(jax.ShapeDtypeStruct((len(TILES), BS, BS), F32), jax.ShapeDtypeStruct(u.shape, F32)),
        in_specs=[VMEM, VMEM, SMEM],
        out_specs=(VMEM, VMEM),
        scratch_shapes=[pltpu.VMEM((3 * BS, width * BS), BF16), pltpu.VMEM((3 * BS, width * BS), BF16)],
        compiler_params=pltpu.CompilerParams(vmem_limit_bytes=40 * 1024 * 1024),
    )(u, blocks, index)


GROUPS = len(TILES) * BS // 8
HALF = GROUPS // 2
PARTS = ((0, 128, "xyz"), (128, 128, "yxz"), (256, 32, "zx"))
SIZES = {"x": X, "y": 4, "z": Z}


def sum_copies():
    total = 2 * len(PARTS)
    for _, _, order in PARTS:
        total += 2 * sum(SIZES[axis] - 1 for axis in order)
    return total + SIZES["y"] - 1


def sum_kernel(g_ref, res, acc, other, bufs, ring, send_sem, recv_sem):
    d, l = lax.axis_index("depth"), lax.axis_index("lat")
    x, z, c = l // (2 * Z), lax.rem(l // 2, Z), lax.rem(l, 2)
    place = {"x": x, "y": d, "z": z}

    def device(axis, index):
        if axis == "y":
            return (index, l)
        if axis == "x":
            return (d, (index * Z + z) * 2 + c)
        return (d, (x * Z + index) * 2 + c)

    twin = (d, l + 1 - 2 * c)
    barrier = pltpu.get_barrier_semaphore()
    greeted = 1
    pl.semaphore_signal(barrier, inc=1, device_id=twin, device_id_type=MESH)
    for axis in "xyz":
        for off in range(1, SIZES[axis]):
            peer = device(axis, lax.rem(place[axis] + off, SIZES[axis]))
            pl.semaphore_signal(barrier, inc=1, device_id=peer, device_id_type=MESH)
            greeted += 1
    pl.semaphore_wait(barrier, greeted)

    used = [0]
    started = []

    def start(src, dst, peer):
        at = used[0]
        used[0] += 1
        copy = pltpu.make_async_remote_copy(
            src_ref=src, dst_ref=dst, send_sem=send_sem.at[at], recv_sem=recv_sem.at[at],
            device_id=peer, device_id_type=MESH,
        )
        copy.start()
        started.append(copy)
        return copy

    mine, theirs = c * HALF, (1 - c) * HALF
    arriving = [start(g_ref.at[pl.ds(theirs + at, n)], other.at[pl.ds(at, n)], twin) for at, n, _ in PARTS]
    state = []
    slot = [0]

    def scatter(part):
        base, n, order, phase = part["base"], part["n"], part["order"], part["phase"]
        axis = order[phase]
        k = SIZES[axis]
        piece = n // k
        here = place[axis]
        copies = []
        for off in range(1, k):
            to = lax.rem(here + off, k)
            room = bufs.at[pl.ds(slot[0], piece)]
            copies.append((start(acc.at[pl.ds(base + to * piece, piece)], room, device(axis, to)), slot[0]))
            slot[0] += piece
        part["wait"] = copies
        part["base"], part["n"], part["phase"] = base + here * piece, piece, phase + 1
        part["path"].append((axis, part["base"], piece))

    def collect(part):
        own = pl.ds(part["base"], part["n"])
        value = acc[own]
        for copy, at in part["wait"]:
            copy.wait_recv()
            value = value + bufs[at : at + part["n"]]
        acc[own] = value

    for at, (copy, (base, n, order)) in enumerate(zip(arriving, PARTS)):
        copy.wait_recv()
        acc[base : base + n] = g_ref[pl.ds(mine + base, n)] + other[base : base + n]
        part = {"base": base, "n": n, "order": order, "phase": 0, "path": []}
        state.append(part)
        scatter(part)
    for phase in range(3):
        for part in state:
            if phase < len(part["order"]):
                collect(part)
                if phase + 1 < len(part["order"]):
                    scatter(part)
    last = state[-1]
    own = pl.ds(last["base"], last["n"])
    ring[d] = acc[own]
    copies = []
    for off in range(1, SIZES["y"]):
        to = lax.rem(d + off, SIZES["y"])
        copies.append(start(acc.at[own], ring.at[d], device("y", to)))
    for copy in copies:
        copy.wait_recv()
    value = ring[0]
    for at in range(1, SIZES["y"]):
        value = value + ring[at]
    res[pl.ds(mine + last["base"], last["n"])] = value
    for part in state[:-1]:
        res[pl.ds(mine + part["base"], part["n"])] = acc[pl.ds(part["base"], part["n"])]

    def gather(part):
        axis, base, n = part["path"][-1]
        part["path"].pop()
        k = SIZES[axis]
        here = place[axis]
        region = res.at[pl.ds(mine + base, n)]
        part["wait"] = []
        for off in range(1, k):
            to = lax.rem(here + off, k)
            part["wait"].append(start(region, region, device(axis, to)))

    for part in state:
        gather(part)
    for _ in range(3):
        for part in state:
            if part["wait"] is None:
                continue
            for copy in part["wait"]:
                copy.wait_recv()
            if part["path"]:
                gather(part)
            else:
                part["wait"] = None
    finals = []
    for base, n, _ in PARTS:
        region = res.at[pl.ds(mine + base, n)]
        finals.append(start(region, region, twin))
    for copy in finals:
        copy.wait_recv()
    for copy in started:
        copy.wait_send()


def sum_everywhere(g):
    copies = sum_copies()
    room = 0
    for _, n, order in PARTS:
        for axis in order:
            n //= SIZES[axis]
            room += (SIZES[axis] - 1) * n
    return pl.pallas_call(
        sum_kernel,
        out_shape=jax.ShapeDtypeStruct((GROUPS, 8, BS), F32),
        in_specs=[VMEM],
        out_specs=VMEM,
        scratch_shapes=[
            pltpu.VMEM((HALF, 8, BS), F32),
            pltpu.VMEM((HALF, 8, BS), F32),
            pltpu.VMEM((room, 8, BS), F32),
            pltpu.VMEM((SIZES["y"], 1, 8, BS), F32),
            pltpu.SemaphoreType.DMA((copies,)),
            pltpu.SemaphoreType.DMA((copies,)),
        ],
        compiler_params=pltpu.CompilerParams(
            collective_id=8, has_side_effects=True, vmem_limit_bytes=40 * 1024 * 1024
        ),
    )(g.reshape(GROUPS, 8, BS))


def tip_kernel(s_ref, tip_ref, out_ref):
    i = pl.program_id(0)
    for j in range(MB):
        cols = slice(j * BS, (j + 1) * BS)

        @pl.when(j <= i)
        def _():
            out_ref[:, cols] = tip_ref[:, cols] - s_ref[i * (i + 1) // 2 + j]

        @pl.when(j > i)
        def _():
            out_ref[:, cols] = tip_ref[:, cols] - s_ref[j * (j + 1) // 2 + i].T


def finish_tip(total, tip):
    n = tip.shape[0]
    return pl.pallas_call(
        tip_kernel,
        grid=(MB,),
        out_shape=jax.ShapeDtypeStruct(tip.shape, F32),
        in_specs=[
            pl.BlockSpec((len(TILES), BS, BS), lambda i: (0, 0, 0)),
            pl.BlockSpec((BS, n), lambda i: (i, 0)),
        ],
        out_specs=pl.BlockSpec((BS, n), lambda i: (i, 0)),
        compiler_params=pltpu.CompilerParams(vmem_limit_bytes=40 * 1024 * 1024),
    )(total.reshape(len(TILES), BS, BS), tip)


def body(diag_blocks, coupling, offsets, arrow_blocks, arrow_index, tip):
    layers = lax.axis_size("depth")
    own = diag_blocks[0]
    incoming = jnp.zeros_like(own)
    for step in range(layers):
        u = factorize(own, incoming)
        handed, incoming = exchange(u, coupling[0], offsets[0], step)
    terms, lower = arrow_terms(u, arrow_blocks[0], arrow_index[0])
    schur_tip = finish_tip(sum_everywhere(terms), tip)
    return (lower[None], handed[None], schur_tip)


def solution(mesh):
    return jax.shard_map(
        body,
        mesh=mesh,
        in_specs=(
            P("depth", "lat", None, None),
            P("depth", "lat", None, None, None),
            P("depth", "lat", None),
            P("depth", "lat", None, None, None),
            P("depth", "lat", None),
            P(),
        ),
        out_specs=(P("depth", "lat", None, None), P("depth", "lat", None, None), P()),
        check_vma=False,
    )
```

time: 807 us -> 188 us (0.23)
  other arithmetic: 359 us -> 0 us
  waiting for transfers between devices: 286 us -> 0 us
  Pallas kernels: 0 us -> 177 us
  matrix products: 67.4 us -> 0 us
  starting transfers between devices: 60 us -> 0 us
  between operations: 15.2 us -> 0.74 us
    another operation x21 -> x0, other arithmetic: 350 us -> none  [the longest x13 190 us: factor_one(): lower_factor = jnp.linalg.cholesky(matrix)]
    psum x1 -> x0, waiting for transfers between devices: 242 us -> none  [body(): schur_tip = tip - lax.psum(term, ('depth', 'lat'))]
    pallas_call x0 -> x11, Pallas kernels: none -> 177 us  [the longest x4 95 us: exchange(): pl.pallas_call(update_kernel, out_shape=(shape, shape), in_specs=[VMEM, V...]
    dot_general x16 -> x0, matrix products: 62.5 us -> none  [the longest x4 14.8 us: schur_update(): return -jnp.einsum('nwba,nwbd->nad', coupling, inner, precision=HIGH)]
    ppermute x19 -> x0, starting transfers between devices: 60 us -> none  [from_behind(): lax.ppermute(value, axis, [(source, source + steps) for source in range(i...]
    ppermute x19 -> x0, waiting for transfers between devices: 43.7 us -> none  [from_behind(): lax.ppermute(value, axis, [(source, source + steps) for source in range(i...]
  transfers between devices with their start and end apart: 20 -> 0, of which waited for: 12 -> 0; matrix products, arithmetic and copies ran while one was open for 1% -> 0% of each run, Pallas kernels for 0% -> 0%
where the time goes in v1:
time: 188 us
  Pallas kernels  177 us (94%)
  local copies, waits for them, and re-layouts  9.6 us (5%)
    pallas_call x4, Pallas kernels, exchange(): pl.pallas_call(update_kernel, out_shape=(shape, shape), in_specs=[VMEM, V...  95 us
    pallas_call x1, Pallas kernels, sum_everywhere(): pl.pallas_call(sum_kernel, out_shape=jax.ShapeDtypeStruct((GROUPS, 8, BS)...  46.2 us
    pallas_call x4, Pallas kernels, factorize(): pl.pallas_call(factor_kernel, out_shape=jax.ShapeDtypeStruct(blocks.shape...  26.9 us
    unnamed x29, local copies, waits for them, and re-layouts  8.88 us
    pallas_call x1, Pallas kernels, finish_tip(): pl.pallas_call(tip_kernel, grid=(MB,), out_shape=jax.ShapeDtypeStruct(tip...  5.6 us

profile of v1, /device:TPU:1, one launch (start us, length us, event | category | flops | bytes accessed | tf_op | source)
XLA Modules:
  0.0 187.8 jit_solution(8210402147518384096)
XLA Ops:
  0.6 0.0 copy-start.12
  0.6 0.7 broadcast_in_dim.9.inc_ref
  1.4 6.7 %shard_map.85.u_ref = f32[4,128,128]{2,1,0:T(8,128)} custom-call(f32[4,128,128]{2,1,0:T(8,128)} %bitcast.22, f32[4,128,128]{2,1,0:T(8,128)} %broadcast_in_dim.9.inc_ref), custom_call_target="tpu_custom_call" | custom-call | tf_op jit(solution)/shard_map/pallas_call | solution.py:110
  8.0 0.0 copy-start
  8.0 1.6 copy-done
  9.6 0.0 copy-start.5
  9.6 0.9 copy-done.5
  10.6 0.0 copy-start.11
  10.6 0.7 copy-done.11
  11.3 0.0 copy-start.1
  11.3 29.9 %shard_map.86 = (f32[4,128,128]{2,1,0:T(8,128)}, f32[4,128,128]{2,1,0:T(8,128)S(1)}) custom-call(f32[4,128,128]{2,1,0:T(8,128)S(1)} %copy-done.5, f32[4,8,128,128]{3,2,1,0:T(8,128)S(1)} %bitcast.9, s32[4,8]{1,0:T(4,128)S(1)} %bitcast.17), custom_call_target="tpu_custom_call" | custom-call | tf_op jit(solution)/shard_map/pallas_call | solution.py:188
  41.2 0.0 copy-start.8
  41.2 0.7 copy-done.8
  41.9 6.7 %shard_map.87.u_ref = f32[4,128,128]{2,1,0:T(8,128)} custom-call(f32[4,128,128]{2,1,0:T(8,128)} %bitcast.23, f32[4,128,128]{2,1,0:T(8,128)} %copy-done.8), custom_call_target="tpu_custom_call" | custom-call | tf_op jit(solution)/shard_map/pallas_call | solution.py:110
  48.5 0.0 copy-done.12
  48.5 0.0 copy-done.1
  48.5 0.0 copy-start.6
  48.6 0.9 copy-done.6
  49.5 22.4 %shard_map.88 = (f32[4,128,128]{2,1,0:T(8,128)}, f32[4,128,128]{2,1,0:T(8,128)S(1)}) custom-call(f32[4,128,128]{2,1,0:T(8,128)S(1)} %copy-done.6, f32[4,8,128,128]{3,2,1,0:T(8,128)S(1)} %bitcast.10, s32[4,8]{1,0:T(4,128)S(1)} %bitcast.18), custom_call_target="tpu_custom_call" | custom-call | tf_op jit(solution)/shard_map/pallas_call | solution.py:188
  71.9 0.0 copy-start.9
  71.9 0.7 copy-done.9
  72.6 6.7 %shard_map.89.u_ref = f32[4,128,128]{2,1,0:T(8,128)} custom-call(f32[4,128,128]{2,1,0:T(8,128)} %bitcast.24, f32[4,128,128]{2,1,0:T(8,128)} %copy-done.9), custom_call_target="tpu_custom_call" | custom-call | tf_op jit(solution)/shard_map/pallas_call | solution.py:110
  79.3 0.0 copy-start.7
  79.3 0.9 copy-done.7
  80.2 0.0 copy-start.4
  80.2 0.0 copy-start.13
  80.3 21.3 %shard_map.90 = (f32[4,128,128]{2,1,0:T(8,128)}, f32[4,128,128]{2,1,0:T(8,128)S(1)}) custom-call(f32[4,128,128]{2,1,0:T(8,128)S(1)} %copy-done.7, f32[4,8,128,128]{3,2,1,0:T(8,128)S(1)} %bitcast.11, s32[4,8]{1,0:T(4,128)S(1)} %bitcast.19), custom_call_target="tpu_custom_call" | custom-call | tf_op jit(solution)/shard_map/pallas_call | solution.py:188
  101.6 0.0 copy-start.10
  101.6 0.7 copy-done.10
  102.3 6.9 %shard_map.91.u_ref = f32[4,128,128]{2,1,0:T(8,128)} custom-call(f32[4,128,128]{2,1,0:T(8,128)} %bitcast.25, f32[4,128,128]{2,1,0:T(8,128)} %copy-done.10), custom_call_target="tpu_custom_call" | custom-call | tf_op jit(solution)/shard_map/pallas_call | solution.py:110
  109.2 0.0 copy-start.3
  109.2 0.9 copy-done.3
  110.1 21.4 %shard_map.93 = (f32[4,128,128]{2,1,0:T(8,128)S(1)}, f32[4,128,128]{2,1,0:T(8,128)}) custom-call(f32[4,128,128]{2,1,0:T(8,128)S(1)} %copy-done.3, f32[4,8,128,128]{3,2,1,0:T(8,128)S(1)} %bitcast.12, s32[4,8]{1,0:T(4,128)S(1)} %bitcast.20), custom_call_target="tpu_custom_call" | custom-call | tf_op jit(solution)/shard_map/pallas_call | solution.py:188
  131.5 0.0 copy-done.4
  131.5 0.0 copy-done.13
  131.6 3.7 %shard_map.92 = (f32[36,128,128]{2,1,0:T(8,128)S(1)}, f32[4,128,128]{2,1,0:T(8,128)}) custom-call(f32[4,128,128]{2,1,0:T(8,128)S(1)} %copy-done.3, f32[4,4,128,128]{3,2,1,0:T(8,128)S(1)} %bitcast.15, s32[4,4]{1,0:T(4,128)S(1)} %bitcast.21), custom_call_target="tpu_custom_call" | custom-call | tf_op jit(solution)/shard_map/pallas_call | solution.py:244
  135.2 0.0 copy-start.2
  135.2 46.2 %shard_map.94 = f32[576,8,128]{2,1,0:T(8,128)S(1)} custom-call(f32[576,8,128]{2,1,0:T(8,128)S(1)} %bitcast.14), custom_call_target="tpu_custom_call" | custom-call | tf_op jit(solution)/shard_map/pallas_call | solution.py:401
  181.4 0.0 copy-done.2
  181.5 5.6 %shard_map.95 = f32[1024,1024]{1,0:T(8,128)} custom-call(f32[36,128,128]{2,1,0:T(8,128)S(1)} %bitcast.13, f32[1024,1024]{1,0:T(8,128)S(1)} %copy-done.2), custom_call_target="tpu_custom_call" | custom-call | tf_op jit(solution)/shard_map/pallas_call | solution.py:436
  187.1 0.7 copy.10
Async XLA Ops:
  0.6 47.9 %copy-start.12 = (s32[1,4,8]{2,1,0:T(4,128)S(1)}, s32[1,4,8]{2,1,0:T(4,128)}, u32[]{:S(2)}) copy-start(s32[1,4,8]{2,1,0:T(4,128)} %param.8) | copy-start | bytes 388
  8.0 1.6 copy-start
  9.6 0.9 copy-start.5
  10.6 0.7 copy-start.11
  11.3 37.3 %copy-start.1 = (f32[1,4,8,128,128]{4,3,2,1,0:T(8,128)S(1)}, f32[1,4,8,128,128]{4,3,2,1,0:T(8,128)}, u32[]{:S(2)}) copy-start(f32[1,4,8,128,128]{4,3,2,1,0:T(8,128)} %param.7) | copy-start | bytes 6291460
  41.2 0.7 copy-start.8
  48.5 1.0 copy-start.6
  71.9 0.7 copy-start.9
  79.3 0.9 copy-start.7
  80.2 51.3 %copy-start.4 = (f32[1,4,4,128,128]{4,3,2,1,0:T(8,128)S(1)}, f32[1,4,4,128,128]{4,3,2,1,0:T(8,128)}, u32[]{:S(2)}) copy-start(f32[1,4,4,128,128]{4,3,2,1,0:T(8,128)} %param.9) | copy-start | bytes 3145732
  80.2 51.3 %copy-start.13 = (s32[1,4,4]{2,1,0:T(4,128)S(1)}, s32[1,4,4]{2,1,0:T(4,128)}, u32[]{:S(2)}) copy-start(s32[1,4,4]{2,1,0:T(4,128)} %param.10) | copy-start | bytes 196
  101.6 0.7 copy-start.10
  109.2 0.9 copy-start.3
  135.2 46.2 %copy-start.2 = (f32[1024,1024]{1,0:T(8,128)S(1)}, f32[1024,1024]{1,0:T(8,128)}, u32[]{:S(2)}) copy-start(f32[1024,1024]{1,0:T(8,128)} %tip_ref.1) | copy-start | bytes 12582916

commit v2 on v0

v2 whole, which is shorter than its diff:
```python
import functools

import jax
import jax.numpy as jnp
from jax import lax
from jax.experimental import pallas as pl
from jax.experimental.pallas import tpu as pltpu
from jax.sharding import PartitionSpec as P

BS = 128
PANEL = 32
PANELS = BS // PANEL
REACH = 8
MB = 8
F32 = jnp.float32
BF16 = jnp.bfloat16
MESH = pl.DeviceIdType.MESH
X, Z = 4, 8
SIZES = {"x": X, "y": 4, "z": Z}
HALF_TILES = 18
HALF = HALF_TILES * 16
PARTS = ((0, 128, "xyz"), (128, 128, "yxz"), (256, 32, "zx"))
TOP = 4


def split2(x):
    high = x.astype(BF16)
    return high, (x - high.astype(F32)).astype(BF16)


def split3(x):
    high = x.astype(BF16)
    rest = x - high.astype(F32)
    middle = rest.astype(BF16)
    return high, middle, (rest - middle.astype(F32)).astype(BF16)


def dot(a, b):
    return jnp.dot(a, b, preferred_element_type=F32)


def dot_t(a, b):
    return lax.dot_general(a, b, (((0,), (0,)), ((), ())), preferred_element_type=F32)


def gram_exact(u, v):
    uh, um, ul = split3(u)
    vh, vm, vl = split3(v)
    return dot_t(
        jnp.concatenate([uh, uh, uh, um, um, ul], 0),
        jnp.concatenate([vh, vm, vl, vh, vm, vh], 0),
    )


def eliminate(part, j0):
    count = part[0].shape[0]
    shape = (count, 8, BS)
    lane = lax.broadcasted_iota(jnp.int32, shape, 2)
    sub = lax.broadcasted_iota(jnp.int32, shape, 1)
    groups = len(part)
    spread = lambda x: jnp.broadcast_to(x, shape)
    for g in range(groups):
        c0 = j0 + 8 * g
        cols = [[spread(part[v][:, :, c0 + k : c0 + k + 1]) for k in range(8)] for v in range(g, groups)]
        keep = (lane < c0) | (lane >= c0 + 8)
        x = jnp.where(keep, part[g], jnp.where(lane == c0 + sub, 1.0, 0.0))
        d = cols[0]
        scales, rows, low = [], [], {}
        for i in range(8):
            scale = lax.rsqrt(spread(d[i][:, i : i + 1, :]))
            li = d[i] * scale
            for k in range(i + 1, 8):
                low[k, i] = spread(li[:, k : k + 1, :])
                d[k] = d[k] - li * low[k, i]
            row = spread(x[:, i : i + 1, :]) * scale
            scales.append(scale)
            rows.append(row)
            x = jnp.where(sub > i, x - li * row, jnp.where(sub == i, row, x))
        for k in range(1, 8):
            for i in range(k):
                x = jnp.where((sub == i) & (lane == c0 + k), low[k, i], x)
        part[g] = x
        for v in range(g + 1, groups):
            d = cols[v - g]
            x = jnp.where(keep, part[v], 0.0)
            for i in range(8):
                mi = d[i] * scales[i]
                for k in range(i + 1, 8):
                    d[k] = d[k] - mi * low[k, i]
                x = x - mi * rows[i]
            part[v] = x
    return jnp.concatenate(part, 1)


def kernel(
    diag_hbm, coup_hbm, off_ref, arrow_hbm, idx_ref, tip_hbm,
    lower_ref, handed_ref, out_ref,
    dbuf, cbuf, bbuf, tbuf, ubuf, corr, landed, window, wide, cwide, bwide, stacked, early, placed, hi, lo,
    g_ref, other, acc, bufs, ring, res,
    load_sem, win_send, win_recv, dep_send, dep_recv, sum_send, sum_recv,
):
    depths, lats = lax.axis_size("depth"), lax.axis_size("lat")
    d, l = lax.axis_index("depth"), lax.axis_index("lat")
    count, width = off_ref.shape
    spokes = idx_ref.shape[1]
    px, pz, c = l // (2 * Z), lax.rem(l // 2, Z), lax.rem(l, 2)
    place = {"x": px, "y": d, "z": pz}
    twin = (d, l + 1 - 2 * c)

    def device(axis, index):
        if axis == "y":
            return (index, l)
        if axis == "x":
            return (d, (index * Z + pz) * 2 + c)
        return (d, (px * Z + index) * 2 + c)

    def lat_at(step):
        return (d, lax.rem(l + step + lats, lats))

    def remote(src, dst, send, recv, peer):
        return pltpu.make_async_remote_copy(
            src_ref=src, dst_ref=dst, send_sem=send, recv_sem=recv, device_id=peer, device_id_type=MESH
        )

    loads = [
        pltpu.make_async_copy(src, dst, load_sem.at[at])
        for at, (src, dst) in enumerate(((diag_hbm, dbuf), (coup_hbm, cbuf), (arrow_hbm, bbuf), (tip_hbm, tbuf)))
    ]
    for load in loads:
        load.start()

    barrier = pltpu.get_barrier_semaphore()
    greeted = 0
    peers = [twin, lat_at(-2), lat_at(2)]
    for axis in "xyz":
        peers += [device(axis, lax.rem(place[axis] + off, SIZES[axis])) for off in range(1, SIZES[axis])]
    for peer in peers:
        pl.semaphore_signal(barrier, inc=1, device_id=peer, device_id_type=MESH)

    def prepare():
        def couple(at, _):
            ch, cl = split2(cbuf[at])
            cwide[at] = jnp.concatenate([ch, ch, cl], 0)
            return 0

        def spoke(n, _):
            for s in range(spokes):
                bh, bl = split2(bbuf[n, s])
                bwide[n, :, s * BS : (s + 1) * BS] = jnp.concatenate([bh, bh, bl], 0)
            placed[n, spokes] = jnp.zeros(placed.shape[2:], BF16)
            return 0

        loads[1].wait()
        loads[2].wait()
        lax.fori_loop(0, count * width, couple, 0)
        lax.fori_loop(0, count, spoke, 0)

    def handed_copy(at):
        if at < TOP:
            rows = (at, pl.ds(0, 2 * PANEL))
        else:
            rows = (slice(None), pl.ds((at - TOP + 2) * PANEL, PANEL))
        return remote(
            handed_ref.at[rows], landed.at[rows], dep_send.at[at], dep_recv.at[at],
            (lax.rem(d + 1, depths), l),
        )

    @pl.when(d == 0)
    def _():
        landed[...] = jnp.zeros_like(landed)

    loads[0].wait()
    pl.semaphore_wait(barrier, len(peers))

    @pl.when(d > 0)
    def _():
        prepare()

    def panel_rows(p):
        return pl.ds(p * PANEL, PANEL)

    def panel_copies(p):
        own = window.at[pl.ds(REACH, count), panel_rows(p)]

        def to(first):
            return window.at[pl.ds(first, count), panel_rows(p)]

        return (
            remote(own, to(4 * count), win_send.at[p, 0], win_recv.at[p, 0], lat_at(-2)),
            remote(own, to(0), win_send.at[p, 1], win_recv.at[p, 1], lat_at(2)),
            remote(own, to(count + 2 * count * c), win_send.at[p, 2], win_recv.at[p, 2], twin),
        )

    def forward_copy(p):
        src = window.at[pl.ds(4 * count - 4 * count * c, count), panel_rows(p)]
        dst = window.at[pl.ds(3 * count - 2 * count * c, count), panel_rows(p)]
        return remote(src, dst, win_send.at[p, 3], win_recv.at[p, 3], twin)

    def forward(p):
        remote(
            window.at[pl.ds(REACH, count), panel_rows(p)],
            window.at[pl.ds(4 * count - 4 * count * c, count), panel_rows(p)],
            win_send.at[p, c], win_recv.at[p, c], twin,
        ).wait_recv()
        forward_copy(p).start()

    def wait_panel(p):
        remote(
            window.at[pl.ds(REACH, count), panel_rows(p)],
            window.at[pl.ds(4 * count * c, count), panel_rows(p)],
            win_send.at[p, 1 - c], win_recv.at[p, 1 - c], twin,
        ).wait_recv()
        panel_copies(p)[2].wait_recv()
        forward_copy(p).wait_recv()

    for p in range(PANELS):
        j0, end = p * PANEL, (p + 1) * PANEL
        needed = {0: range(TOP), 2: (TOP,), 3: (TOP + 1,)}.get(p, ())
        if needed:

            @pl.when(d > 0)
            def _():
                for at in needed:
                    handed_copy(at).wait_recv()

        a = dbuf[:, j0:end, :] + landed[:, j0:end, :]
        lane = lax.broadcasted_iota(jnp.int32, a.shape, 2)
        row = j0 + lax.broadcasted_iota(jnp.int32, a.shape, 1)
        if p:
            a = jnp.where(lane < j0, 0.0, a) - corr[:, j0:end, :]
        u = eliminate([a[:, 8 * v : 8 * v + 8] for v in range(PANEL // 8)], j0)
        ubuf[:, j0:end, :] = u
        window[REACH : REACH + count, j0:end, :] = jnp.where(lane <= row, u, 0.0)
        for copy in panel_copies(p):
            copy.start()
        if end < BS:
            right = jnp.where((lane < end) & (lane > row), 0.0, u)
            for m in range(count):
                full = gram_exact(u[m], right[m])[end:]
                if p:
                    old = corr[m, end:, :]
                    ln = lax.broadcasted_iota(jnp.int32, old.shape, 1)
                    full = full + jnp.where((ln >= j0) & (ln < end), 0.0, old)
                corr[m, end:, :] = full
        if p == 2:
            forward(0)

    def update(ranges, hand_on):
        forward(1)
        arrived = 0
        for stage, (first, last) in enumerate(ranges):
            if last == 2 * PANEL:
                pass
            elif arrived < 3:
                forward(2)
                forward(3)
                arrived = 3
            for p in range(first // PANEL, last // PANEL):
                wait_panel(p)
            rows = last - first
            for step in range(-2, 3):
                at = REACH + step * count
                inside = (l + step >= 0) & (l + step < lats)
                high, low = split2(jnp.where(inside, window[at : at + count, first:last, :], 0.0))
                wide[at : at + count, first:last, :] = jnp.concatenate([high, low, high], 2)
            for m in range(count):
                for w in range(width):
                    x = dot(wide[off_ref[m, w] + (m + REACH), first:last, :], cwide[m * width + w])
                    xh, xl = split2(x)
                    stacked[w * rows : (w + 1) * rows, :] = jnp.concatenate([xh, xl], 1)
                both = dot_t(stacked[: width * rows, :BS], stacked[: width * rows, :])
                if stage:
                    both = both + early[m]
                if stage + 1 < len(ranges):
                    early[m] = both
                else:
                    cross = both[:, BS:]
                    handed_ref[m] = -(both[:, :BS] + cross + cross.T)
                    if hand_on:
                        handed_copy(m).start()
        if hand_on:
            handed_copy(TOP).start()
            handed_copy(TOP + 1).start()

    @pl.when(d == 0)
    def _():
        prepare()

    @pl.when(d < depths - 1)
    def _():
        update(((0, 2 * PANEL), (2 * PANEL, 3 * PANEL), (3 * PANEL, BS)), True)

    row = lax.broadcasted_iota(jnp.int32, (BS, BS), 0)
    col = lax.broadcasted_iota(jnp.int32, (BS, BS), 1)
    for n in range(count):
        high, low = split2(jnp.where(col <= row, ubuf[n], 0.0))
        t = dot(jnp.concatenate([high, low, high], 1), bwide[n])
        for s in range(spokes):
            th, tl = split2(t[:, s * BS : (s + 1) * BS])
            placed[n, s, 0] = th
            placed[n, s, 1] = tl
    for n in range(count):
        for m in range(MB):
            slot = spokes
            for s in range(spokes):
                slot = jnp.where(idx_ref[n, s] == m, s, slot)
            both = placed[n, slot]
            for at in (m, m + MB)[: 2 if m < MB // 2 else 1]:
                hi[n * BS : (n + 1) * BS, at * BS : (at + 1) * BS] = both[0]
                lo[n * BS : (n + 1) * BS, at * BS : (at + 1) * BS] = both[1]

    def tile_product(i, first, tiles):
        left = pl.ds(pl.multiple_of(i * BS, BS), BS)
        right = pl.ds(pl.multiple_of(first * BS, BS), tiles * BS)
        return dot_t(hi[:, left], hi[:, right]) + dot_t(hi[:, left], lo[:, right]) + dot_t(lo[:, left], hi[:, right])

    def put(h, k, value):
        g_ref[pl.ds((h * HALF_TILES + k) * 16, 16)] = value.reshape(16, 8, BS)

    def half_products(h):
        for ii in range(4):
            product = tile_product(4 * h + ii, 4 * h + ii, 4)
            for delta in range(4):
                put(h, delta * 4 + ii, product[:, delta * BS : (delta + 1) * BS])
        for ii in range(2):
            put(h, 16 + ii, tile_product(2 * h + ii, 2 * h + ii + 4, 1))

    used = [0]
    started = []

    def start(src, dst, peer):
        at = used[0]
        used[0] += 1
        copy = remote(src, dst, sum_send.at[at], sum_recv.at[at], peer)
        copy.start()
        started.append(copy)
        return copy

    mine, theirs = c * HALF, (1 - c) * HALF
    half_products(1 - c)
    arriving = [start(g_ref.at[pl.ds(theirs + at, n)], other.at[pl.ds(at, n)], twin) for at, n, _ in PARTS]
    half_products(c)
    slot = [0]

    def scatter(part):
        axis = part["order"][part["phase"]]
        k, here = SIZES[axis], place[axis]
        base, piece = part["base"], part["n"] // k
        part["wait"] = []
        for off in range(1, k):
            to = lax.rem(here + off, k)
            copy = start(
                acc.at[pl.ds(base + to * piece, piece)], bufs.at[pl.ds(slot[0], piece)], device(axis, to)
            )
            part["wait"].append((copy, slot[0]))
            slot[0] += piece
        part["base"], part["n"], part["phase"] = base + here * piece, piece, part["phase"] + 1
        part["path"].append((axis, part["base"], piece))

    def collect(part):
        own = pl.ds(part["base"], part["n"])
        value = acc[own]
        for copy, at in part["wait"]:
            copy.wait_recv()
            value = value + bufs[at : at + part["n"]]
        acc[own] = value

    state = []
    for copy, (base, n, order) in zip(arriving, PARTS):
        copy.wait_recv()
        acc[base : base + n] = g_ref[pl.ds(mine + base, n)] + other[base : base + n]
        part = {"base": base, "n": n, "order": order, "phase": 0, "path": []}
        state.append(part)
        scatter(part)

    for n in range(count):
        u = ubuf[n]
        lower_ref[n] = jnp.where(col > row, u, jnp.where(col == row, 1.0 / u, 0.0)).T

    @pl.when(d == depths - 1)
    def _():
        update(((0, BS),), False)

    for phase in range(3):
        for part in state:
            if phase < len(part["order"]):
                collect(part)
                if phase + 1 < len(part["order"]):
                    scatter(part)
    last = state[-1]
    own = pl.ds(last["base"], last["n"])
    ring[d] = acc[own]
    copies = []
    for off in range(1, SIZES["y"]):
        to = lax.rem(d + off, SIZES["y"])
        copies.append(start(acc.at[own], ring.at[d], device("y", to)))
    for part in state[:-1]:
        res[pl.ds(mine + part["base"], part["n"])] = acc[pl.ds(part["base"], part["n"])]

    def gather(part):
        axis, base, n = part["path"].pop()
        k, here = SIZES[axis], place[axis]
        region = res.at[pl.ds(mine + base, n)]
        part["wait"] = [start(region, region, device(axis, lax.rem(here + off, k))) for off in range(1, k)]

    for part in state[:-1]:
        gather(part)
    for copy in copies:
        copy.wait_recv()
    value = ring[0]
    for at in range(1, SIZES["y"]):
        value = value + ring[at]
    res[pl.ds(mine + last["base"], last["n"])] = value
    gather(last)

    def emit(h, first, tiles):
        def one(k, _):
            i = jnp.where(k < 16, 4 * h + lax.rem(k, 4), 2 * h + k - 16)
            j = lax.rem(i + k // 4, MB)
            rows, cols = pl.ds(pl.multiple_of(i * BS, BS), BS), pl.ds(pl.multiple_of(j * BS, BS), BS)
            value = res[pl.ds((h * HALF_TILES + k) * 16, 16)].reshape(BS, BS)
            out_ref[rows, cols] = tbuf[rows, cols] - value

            @pl.when(k >= 4)
            def _():
                out_ref[cols, rows] = tbuf[cols, rows] - value.T

            return 0

        lax.fori_loop(first, first + tiles, one, 0)

    finals = []
    for _ in range(3):
        for part, (base, n, _) in zip(state, PARTS):
            if part["wait"] is None:
                continue
            for copy in part["wait"]:
                copy.wait_recv()
            if part["path"]:
                gather(part)
            else:
                part["wait"] = None
                region = res.at[pl.ds(mine + base, n)]
                finals.append((start(region, region, twin), base // 16, n // 16))
    loads[3].wait()
    for _, first, tiles in finals:
        emit(c, first, tiles)
    for copy, first, tiles in finals:
        copy.wait_recv()
        emit(1 - c, first, tiles)

    for copy in started:
        copy.wait_send()
    for p in range(PANELS):
        for copy in panel_copies(p):
            copy.wait_send()
        forward_copy(p).wait_send()

    @pl.when(d < depths - 1)
    def _():
        for at in range(TOP + 2):
            handed_copy(at).wait_send()


def body(diag_blocks, coupling, offsets, arrow_blocks, arrow_index, tip):
    count, width = offsets.shape[1:]
    spokes = arrow_index.shape[2]
    copies, room = 2 * len(PARTS) + SIZES["y"] - 1, 0
    for _, n, order in PARTS:
        for axis in order:
            n //= SIZES[axis]
            room += (SIZES[axis] - 1) * n
            copies += 2 * (SIZES[axis] - 1)
    vmem, smem, hbm = (pl.BlockSpec(memory_space=space) for space in (pltpu.VMEM, pltpu.SMEM, pl.ANY))
    blocks = jax.ShapeDtypeStruct((count, BS, BS), F32)
    band = 2 * REACH + count
    dma = pltpu.SemaphoreType.DMA
    lower, handed, schur_tip = pl.pallas_call(
        kernel,
        out_shape=(blocks, blocks, jax.ShapeDtypeStruct(tip.shape, F32)),
        in_specs=[hbm, hbm, smem, hbm, smem, hbm],
        out_specs=(vmem, vmem, vmem),
        scratch_shapes=[
            pltpu.VMEM((count, BS, BS), F32),
            pltpu.VMEM((count * width, BS, BS), F32),
            pltpu.VMEM((count, spokes, BS, BS), F32),
            pltpu.VMEM(tip.shape, F32),
            pltpu.VMEM((count, BS, BS), F32),
            pltpu.VMEM((count, BS, BS), F32),
            pltpu.VMEM((count, BS, BS), F32),
            pltpu.VMEM((band, BS, BS), F32),
            pltpu.VMEM((band, BS, 3 * BS), BF16),
            pltpu.VMEM((count * width, 3 * BS, BS), BF16),
            pltpu.VMEM((count, 3 * BS, spokes * BS), BF16),
            pltpu.VMEM((width * BS, 2 * BS), BF16),
            pltpu.VMEM((count, BS, 2 * BS), F32),
            pltpu.VMEM((count, spokes + 1, 2, BS, BS), BF16),
            pltpu.VMEM((count * BS, 12 * BS), BF16),
            pltpu.VMEM((count * BS, 12 * BS), BF16),
            pltpu.VMEM((2 * HALF, 8, BS), F32),
            pltpu.VMEM((HALF, 8, BS), F32),
            pltpu.VMEM((HALF, 8, BS), F32),
            pltpu.VMEM((room, 8, BS), F32),
            pltpu.VMEM((SIZES["y"], 1, 8, BS), F32),
            pltpu.VMEM((2 * HALF, 8, BS), F32),
            dma((4,)),
            dma((PANELS, 4)),
            dma((PANELS, 4)),
            dma((TOP + 2,)),
            dma((TOP + 2,)),
            dma((copies,)),
            dma((copies,)),
        ],
        compiler_params=pltpu.CompilerParams(
            collective_id=0, has_side_effects=True, vmem_limit_bytes=56 * 1024 * 1024
        ),
    )(diag_blocks[0], coupling[0].reshape(count * width, BS, BS), offsets[0], arrow_blocks[0], arrow_index[0], tip)
    return (lower[None], handed[None], schur_tip)


def solution(mesh):
    return jax.shard_map(
        body,
        mesh=mesh,
        in_specs=(
            P("depth", "lat", None, None),
            P("depth", "lat", None, None, None),
            P("depth", "lat", None),
            P("depth", "lat", None, None, None),
            P("depth", "lat", None),
            P(),
        ),
        out_specs=(P("depth", "lat", None, None), P("depth", "lat", None, None), P()),
        check_vma=False,
    )
```

time: 807 us -> 125 us (0.15)
  other arithmetic: 359 us -> 0 us
  waiting for transfers between devices: 286 us -> 0 us
  Pallas kernels: 0 us -> 116 us
  matrix products: 67.4 us -> 0 us
  starting transfers between devices: 60 us -> 0 us
  between operations: 15.2 us -> 0.64 us
    another operation x21 -> x0, other arithmetic: 350 us -> none  [the longest x13 190 us: factor_one(): lower_factor = jnp.linalg.cholesky(matrix)]
    psum x1 -> x0, waiting for transfers between devices: 242 us -> none  [body(): schur_tip = tip - lax.psum(term, ('depth', 'lat'))]
    pallas_call x0 -> x1, Pallas kernels: none -> 116 us  [body(): pl.pallas_call(kernel, out_shape=(blocks, blocks, jax.ShapeDtypeStruct(ti...]
    dot_general x16 -> x0, matrix products: 62.5 us -> none  [the longest x4 14.8 us: schur_update(): return -jnp.einsum('nwba,nwbd->nad', coupling, inner, precision=HIGH)]
    ppermute x19 -> x0, starting transfers between devices: 60 us -> none  [from_behind(): lax.ppermute(value, axis, [(source, source + steps) for source in range(i...]
    ppermute x19 -> x0, waiting for transfers between devices: 43.7 us -> none  [from_behind(): lax.ppermute(value, axis, [(source, source + steps) for source in range(i...]
  transfers between devices with their start and end apart: 20 -> 0, of which waited for: 12 -> 0; matrix products, arithmetic and copies ran while one was open for 1% -> 0% of each run, Pallas kernels for 0% -> 0%
where the time goes in v2:
time: 125 us; the launch traced here: 124 us
  Pallas kernels  116 us (93%)
  local copies, waits for them, and re-layouts  8.13 us (7%)
    pallas_call x1, Pallas kernels, body(): pl.pallas_call(kernel, out_shape=(blocks, blocks, jax.ShapeDtypeStruct(ti...  116 us
    unnamed x3, local copies, waits for them, and re-layouts  8.13 us

profile of v2, /device:TPU:1, one launch (start us, length us, event | category | flops | bytes accessed | tf_op | source)
XLA Modules:
  0.0 124.3 jit_solution(16111579492199710335)
XLA Ops:
  0.6 115.5 %shard_map.85 = (f32[4,128,128]{2,1,0:T(8,128)}, f32[4,128,128]{2,1,0:T(8,128)}, f32[1024,1024]{1,0:T(8,128)}) custom-call(f32[4,128,128]{2,1,0:T(8,128)} %bitcast.9, f32[32,128,128]{2,1,0:T(8,128)} %bitcast.7, s32[4,8]{1,0:T(4,128)} %bitcast.12, f32[4,4,128,128]{3,2,1,0:T(8,128)} %bitcast.8, s32[4,4]{1,0:T(4,128)} %bitcast.13, f32[1024,1024]{1,0:T(8,128)} %tip_hbm.1), custom_call_target="tpu_custom_call" | custom-call | tf_op jit(solution)/shard_map/pallas_call | solution.py:478
  116.2 1.7 %copy.12 = f32[1,4,128,128]{3,2,1,0:T(8,128)} copy(f32[1,4,128,128]{3,2,1,0:T(8,128)} %bitcast.11) | data formatting | bytes 524288
  117.9 1.7 %copy.13 = f32[1,4,128,128]{3,2,1,0:T(8,128)} copy(f32[1,4,128,128]{3,2,1,0:T(8,128)} %bitcast.10) | data formatting | bytes 524288
  119.5 4.8 %copy.14 = f32[1024,1024]{1,0:T(8,128)} copy(f32[1024,1024]{1,0:T(8,128)} %get-tuple-element.14) | data formatting | bytes 8388608

commit v3 on v2

--- a/solution.py
+++ b/solution.py
@@ -20,7 +20,8 @@
 HALF_TILES = 18
 HALF = HALF_TILES * 16
 PARTS = ((0, 128, "xyz"), (128, 128, "yxz"), (256, 32, "zx"))
-TOP = 4
+PIECES = ((64, 0, 2, 0, 32), (80, 1, 4, 0, 16), (96, 1, 4, 16, 32), (112, 2, 4, 0, 16), (128, 2, 4, 16, 32))
+RELAYED = 3
 
 
 def split2(x):
@@ -52,7 +53,7 @@
     )
 
 
-def eliminate(part, j0):
+def eliminate(part, j0, done):
     count = part[0].shape[0]
     shape = (count, 8, BS)
     lane = lax.broadcasted_iota(jnp.int32, shape, 2)
@@ -89,15 +90,15 @@
                     d[k] = d[k] - mi * low[k, i]
                 x = x - mi * rows[i]
             part[v] = x
-    return jnp.concatenate(part, 1)
+        done(g)
 
 
 def kernel(
-    diag_hbm, coup_hbm, off_ref, arrow_hbm, idx_ref, tip_hbm,
-    lower_ref, handed_ref, out_ref,
-    dbuf, cbuf, bbuf, tbuf, ubuf, corr, landed, window, wide, cwide, bwide, stacked, early, placed, hi, lo,
+    diag_hbm, coup_hbm, off_ref, arrow_hbm, idx_ref,
+    ubuf, handed_ref, res_hbm,
+    dbuf, cbuf, bbuf, corr, landed, halves, thirds, fourths, wide, cwide, bwide, stacked, early, placed, hi, lo,
     g_ref, other, acc, bufs, ring, res,
-    load_sem, win_send, win_recv, dep_send, dep_recv, sum_send, sum_recv,
+    load_sem, store_sem, win_send, win_recv, dep_send, dep_recv, sum_send, sum_recv,
 ):
     depths, lats = lax.axis_size("depth"), lax.axis_size("lat")
     d, l = lax.axis_index("depth"), lax.axis_index("lat")
@@ -124,14 +125,13 @@
 
     loads = [
         pltpu.make_async_copy(src, dst, load_sem.at[at])
-        for at, (src, dst) in enumerate(((diag_hbm, dbuf), (coup_hbm, cbuf), (arrow_hbm, bbuf), (tip_hbm, tbuf)))
+        for at, (src, dst) in enumerate(((diag_hbm, dbuf), (coup_hbm, cbuf), (arrow_hbm, bbuf)))
     ]
     for load in loads:
         load.start()
 
     barrier = pltpu.get_barrier_semaphore()
-    greeted = 0
-    peers = [twin, lat_at(-2), lat_at(2)]
+    peers = [twin, lat_at(-2), lat_at(2), lat_at(2 * c - 1)]
     for axis in "xyz":
         peers += [device(axis, lax.rem(place[axis] + off, SIZES[axis])) for off in range(1, SIZES[axis])]
     for peer in peers:
@@ -156,10 +156,10 @@
         lax.fori_loop(0, count, spoke, 0)
 
     def handed_copy(at):
-        if at < TOP:
-            rows = (at, pl.ds(0, 2 * PANEL))
+        if at < count:
+            rows = (at, pl.ds(0, PANEL))
         else:
-            rows = (slice(None), pl.ds((at - TOP + 2) * PANEL, PANEL))
+            rows = (slice(None), pl.ds((at - count + 1) * PANEL, PANEL))
         return remote(
             handed_ref.at[rows], landed.at[rows], dep_send.at[at], dep_recv.at[at],
             (lax.rem(d + 1, depths), l),
@@ -170,70 +170,120 @@
         landed[...] = jnp.zeros_like(landed)
 
     loads[0].wait()
-    pl.semaphore_wait(barrier, len(peers))
 
     @pl.when(d > 0)
     def _():
         prepare()
 
-    def panel_rows(p):
-        return pl.ds(p * PANEL, PANEL)
-
-    def panel_copies(p):
-        own = window.at[pl.ds(REACH, count), panel_rows(p)]
-
-        def to(first):
-            return window.at[pl.ds(first, count), panel_rows(p)]
-
-        return (
-            remote(own, to(4 * count), win_send.at[p, 0], win_recv.at[p, 0], lat_at(-2)),
-            remote(own, to(0), win_send.at[p, 1], win_recv.at[p, 1], lat_at(2)),
-            remote(own, to(count + 2 * count * c), win_send.at[p, 2], win_recv.at[p, 2], twin),
-        )
-
-    def forward_copy(p):
-        src = window.at[pl.ds(4 * count - 4 * count * c, count), panel_rows(p)]
-        dst = window.at[pl.ds(3 * count - 2 * count * c, count), panel_rows(p)]
-        return remote(src, dst, win_send.at[p, 3], win_recv.at[p, 3], twin)
-
-    def forward(p):
-        remote(
-            window.at[pl.ds(REACH, count), panel_rows(p)],
-            window.at[pl.ds(4 * count - 4 * count * c, count), panel_rows(p)],
-            win_send.at[p, c], win_recv.at[p, c], twin,
-        ).wait_recv()
-        forward_copy(p).start()
-
-    def wait_panel(p):
-        remote(
-            window.at[pl.ds(REACH, count), panel_rows(p)],
-            window.at[pl.ds(4 * count * c, count), panel_rows(p)],
-            win_send.at[p, 1 - c], win_recv.at[p, 1 - c], twin,
-        ).wait_recv()
-        panel_copies(p)[2].wait_recv()
-        forward_copy(p).wait_recv()
+    arrived = (halves, thirds, fourths)
+
+    def place_of(step, p):
+        _, buffer, blocks, first, last = PIECES[p]
+        return arrived[buffer].at[pl.ds(step * blocks, blocks), pl.ds(first, last - first)]
+
+    def received(p, at, step):
+        return remote(place_of(2, p), place_of(step, p), win_send.at[p, at], win_recv.at[p, at], twin)
+
+    def piece_copies(p):
+        own = place_of(2, p)
+        copies = [
+            remote(own, place_of(4, p), win_send.at[p, 0], win_recv.at[p, 0], lat_at(-2)),
+            remote(own, place_of(0, p), win_send.at[p, 1], win_recv.at[p, 1], lat_at(2)),
+            remote(own, place_of(1 + 2 * c, p), win_send.at[p, 2], win_recv.at[p, 2], twin),
+        ]
+        if p >= RELAYED:
+            copies.append(crossing(p))
+        return copies
+
+    def crossing(p):
+        if p < RELAYED:
+            src, peer = place_of(4 - 4 * c, p), twin
+        else:
+            src, peer = place_of(2, p), lat_at(2 * c - 1)
+        return remote(src, place_of(3 - 2 * c, p), win_send.at[p, 3], win_recv.at[p, 3], peer)
+
+    def hand_over(p):
+        received(p, c, 4 - 4 * c).wait_recv()
+        if p < RELAYED:
+            crossing(p).start()
+
+    def wait_piece(p):
+        received(p, 1 - c, 4 * c).wait_recv()
+        received(p, 2, 1 + 2 * c).wait_recv()
+        crossing(p).wait_recv()
+
+    def pack(p):
+        end, buffer, blocks, first, last = PIECES[p]
+        rows = end - (last - first)
+        value = ubuf[:, rows:end, :]
+        lane = lax.broadcasted_iota(jnp.int32, value.shape, 2)
+        value = jnp.where(lane <= rows + lax.broadcasted_iota(jnp.int32, value.shape, 1), value, 0.0)
+        if buffer == 0:
+            half = lane[:2] < BS // 2
+            value = jnp.where(half, value[:2], pltpu.roll(value[2:], BS // 2, 2))
+        elif buffer == 1:
+            top = ubuf[:, first:last, :]
+            top = jnp.where(lane <= first + lax.broadcasted_iota(jnp.int32, top.shape, 1), top, 0.0)
+            value = jnp.where(lane < BS - PANEL, value, pltpu.roll(top, BS - PANEL, 2))
+        arrived[buffer][2 * blocks : 3 * blocks, first:last, :] = value
+
+    def widen(rows, blocks, value):
+        high, low = split2(value)
+        wide[blocks, rows, :] = jnp.concatenate([high, low, high], 2)
+
+    def unpack(buffers):
+        for step in range(5):
+            inside = (l + step >= 2) & (l + step < lats + 2)
+            at = step * count
+            for buffer in buffers:
+                blocks = 2 if buffer == 0 else count
+                value = jnp.where(inside, arrived[buffer][step * blocks : (step + 1) * blocks], 0.0)
+                lane = lax.broadcasted_iota(jnp.int32, value.shape, 2)
+                if buffer == 0:
+                    half = lane < BS // 2
+                    widen(slice(32, 64), slice(at, at + 2), jnp.where(half, value, 0.0))
+                    widen(slice(32, 64), slice(at + 2, at + 4), jnp.where(half, pltpu.roll(value, BS // 2, 2), 0.0))
+                elif buffer == 1:
+                    widen(slice(64, 96), slice(at, at + count), jnp.where(lane < BS - PANEL, value, 0.0))
+                    top = jnp.where(lane < PANEL, pltpu.roll(value, PANEL, 2), 0.0)
+                    widen(slice(0, 32), slice(at, at + count), top)
+                else:
+                    widen(slice(96, 128), slice(at, at + count), value)
 
     for p in range(PANELS):
         j0, end = p * PANEL, (p + 1) * PANEL
-        needed = {0: range(TOP), 2: (TOP,), 3: (TOP + 1,)}.get(p, ())
-        if needed:
-
-            @pl.when(d > 0)
-            def _():
-                for at in needed:
-                    handed_copy(at).wait_recv()
+        needed = (count + p - 1,) if p else range(count)
+
+        @pl.when(d > 0)
+        def _():
+            for at in needed:
+                handed_copy(at).wait_recv()
 
         a = dbuf[:, j0:end, :] + landed[:, j0:end, :]
         lane = lax.broadcasted_iota(jnp.int32, a.shape, 2)
         row = j0 + lax.broadcasted_iota(jnp.int32, a.shape, 1)
         if p:
             a = jnp.where(lane < j0, 0.0, a) - corr[:, j0:end, :]
-        u = eliminate([a[:, 8 * v : 8 * v + 8] for v in range(PANEL // 8)], j0)
-        ubuf[:, j0:end, :] = u
-        window[REACH : REACH + count, j0:end, :] = jnp.where(lane <= row, u, 0.0)
-        for copy in panel_copies(p):
-            copy.start()
+        part = [a[:, 8 * v : 8 * v + 8] for v in range(PANEL // 8)]
+
+        def done(g):
+            if g % 2 == 0:
+                return
+            row = j0 + 8 * g - 8
+            ubuf[:, row : row + 16, :] = jnp.concatenate(part[g - 1 : g + 1], 1)
+            for at, piece in enumerate(PIECES):
+                if piece[0] == row + 16:
+                    pack(at)
+                    if at == 0:
+                        pl.semaphore_wait(barrier, len(peers))
+                    for copy in piece_copies(at):
+                        copy.start()
+            if row + 16 == PIECES[3][0]:
+                hand_over(0)
+
+        eliminate(part, j0, done)
         if end < BS:
+            u = jnp.concatenate(part, 1)
             right = jnp.where((lane < end) & (lane > row), 0.0, u)
             for m in range(count):
                 full = gram_exact(u[m], right[m])[end:]
@@ -242,27 +292,21 @@
                     ln = lax.broadcasted_iota(jnp.int32, old.shape, 1)
                     full = full + jnp.where((ln >= j0) & (ln < end), 0.0, old)
                 corr[m, end:, :] = full
-        if p == 2:
-            forward(0)
 
     def update(ranges, hand_on):
-        forward(1)
-        arrived = 0
+        for p in range(1, RELAYED):
+            hand_over(p)
         for stage, (first, last) in enumerate(ranges):
-            if last == 2 * PANEL:
-                pass
-            elif arrived < 3:
-                forward(2)
-                forward(3)
-                arrived = 3
-            for p in range(first // PANEL, last // PANEL):
-                wait_panel(p)
             rows = last - first
-            for step in range(-2, 3):
-                at = REACH + step * count
-                inside = (l + step >= 0) & (l + step < lats)
-                high, low = split2(jnp.where(inside, window[at : at + count, first:last, :], 0.0))
-                wide[at : at + count, first:last, :] = jnp.concatenate([high, low, high], 2)
+            if first == 0:
+                for p in range(RELAYED):
+                    wait_piece(p)
+                unpack((0, 1))
+            if last == BS:
+                for p in range(RELAYED, len(PIECES)):
+                    hand_over(p)
+                    wait_piece(p)
+                unpack((2,))
             for m in range(count):
                 for w in range(width):
                     x = dot(wide[off_ref[m, w] + (m + REACH), first:last, :], cwide[m * width + w])
@@ -279,8 +323,8 @@
                     if hand_on:
                         handed_copy(m).start()
         if hand_on:
-            handed_copy(TOP).start()
-            handed_copy(TOP + 1).start()
+            for p in range(1, PANELS):
+                handed_copy(count + p - 1).start()
 
     @pl.when(d == 0)
     def _():
@@ -288,7 +332,7 @@
 
     @pl.when(d < depths - 1)
     def _():
-        update(((0, 2 * PANEL), (2 * PANEL, 3 * PANEL), (3 * PANEL, BS)), True)
+        update(((0, 96), (96, 128)), True)
 
     row = lax.broadcasted_iota(jnp.int32, (BS, BS), 0)
     col = lax.broadcasted_iota(jnp.int32, (BS, BS), 1)
@@ -373,10 +417,6 @@
         state.append(part)
         scatter(part)
 
-    for n in range(count):
-        u = ubuf[n]
-        lower_ref[n] = jnp.where(col > row, u, jnp.where(col == row, 1.0 / u, 0.0)).T
-
     @pl.when(d == depths - 1)
     def _():
         update(((0, BS),), False)
@@ -413,21 +453,11 @@
     res[pl.ds(mine + last["base"], last["n"])] = value
     gather(last)
 
-    def emit(h, first, tiles):
-        def one(k, _):
-            i = jnp.where(k < 16, 4 * h + lax.rem(k, 4), 2 * h + k - 16)
-            j = lax.rem(i + k // 4, MB)
-            rows, cols = pl.ds(pl.multiple_of(i * BS, BS), BS), pl.ds(pl.multiple_of(j * BS, BS), BS)
-            value = res[pl.ds((h * HALF_TILES + k) * 16, 16)].reshape(BS, BS)
-            out_ref[rows, cols] = tbuf[rows, cols] - value
-
-            @pl.when(k >= 4)
-            def _():
-                out_ref[cols, rows] = tbuf[cols, rows] - value.T
-
-            return 0
-
-        lax.fori_loop(first, first + tiles, one, 0)
+    def store(at, half, base, n):
+        groups = pl.ds(half + base, n)
+        copy = pltpu.make_async_copy(res.at[groups], res_hbm.at[groups], store_sem.at[at])
+        copy.start()
+        return copy
 
     finals = []
     for _ in range(3):
@@ -441,25 +471,79 @@
             else:
                 part["wait"] = None
                 region = res.at[pl.ds(mine + base, n)]
-                finals.append((start(region, region, twin), base // 16, n // 16))
-    loads[3].wait()
-    for _, first, tiles in finals:
-        emit(c, first, tiles)
-    for copy, first, tiles in finals:
+                finals.append((start(region, region, twin), base, n))
+    stores = []
+    for _, base, n in finals:
+        stores.append(store(len(stores), mine, base, n))
+    for copy, base, n in finals:
         copy.wait_recv()
-        emit(1 - c, first, tiles)
-
+        stores.append(store(len(stores), theirs, base, n))
+
+    for copy in stores:
+        copy.wait()
     for copy in started:
         copy.wait_send()
-    for p in range(PANELS):
-        for copy in panel_copies(p):
+    for p in range(len(PIECES)):
+        for copy in piece_copies(p):
             copy.wait_send()
-        forward_copy(p).wait_send()
+        if p < RELAYED:
+            crossing(p).wait_send()
 
     @pl.when(d < depths - 1)
     def _():
-        for at in range(TOP + 2):
+        for at in range(count + PANELS - 1):
             handed_copy(at).wait_send()
+
+
+def tile_of(i, j):
+    delta = (j - i) % MB
+    if delta > MB // 2 or (delta == MB // 2 and i >= MB // 2):
+        return tile_of(j, i)[0], True
+    if delta == MB // 2:
+        return (i // 2) * HALF_TILES + 16 + i % 2, False
+    return (i // 4) * HALF_TILES + delta * 4 + i % 4, False
+
+
+def finish_kernel(
+    u_hbm, handed_hbm, res_hbm, tip_hbm, lower_hbm, given_hbm, out_hbm,
+    u, handed, res, tip, lower, out, sems, row_sems, out_sems,
+):
+    load_u = pltpu.make_async_copy(u_hbm, u, sems.at[0])
+    load_handed = pltpu.make_async_copy(handed_hbm, handed, sems.at[1])
+    load_res = [
+        pltpu.make_async_copy(res_hbm.at[pl.ds(h * HALF, HALF)], res.at[pl.ds(h * HALF, HALF)], sems.at[2 + h])
+        for h in range(2)
+    ]
+    kept = pltpu.make_async_copy(lower, lower_hbm, sems.at[4])
+    given = pltpu.make_async_copy(handed, given_hbm, sems.at[5])
+    row_loads, row_stores = [], []
+    for i in range(MB):
+        rows = pl.ds(i * BS, BS)
+        row_loads.append(pltpu.make_async_copy(tip_hbm.at[rows], tip.at[rows], row_sems.at[i]))
+        row_stores.append(pltpu.make_async_copy(out.at[rows], out_hbm.at[rows], out_sems.at[i]))
+    for copy in [load_u, load_handed, *load_res, *row_loads]:
+        copy.start()
+    row = lax.broadcasted_iota(jnp.int32, (BS, BS), 0)
+    col = lax.broadcasted_iota(jnp.int32, (BS, BS), 1)
+    load_u.wait()
+    for n in range(u.shape[0]):
+        un = u[n]
+        lower[n] = jnp.where(col > row, un, jnp.where(col == row, 1.0 / un, 0.0)).T
+    kept.start()
+    load_handed.wait()
+    given.start()
+    for copy in load_res:
+        copy.wait()
+    for i in range(MB):
+        row_loads[i].wait()
+        for j in range(MB):
+            at, turned = tile_of(i, j)
+            value = res[at * 16 : at * 16 + 16].reshape(BS, BS)
+            here = (slice(i * BS, i * BS + BS), slice(j * BS, j * BS + BS))
+            out[here] = tip[here] - (value.T if turned else value)
+        row_stores[i].start()
+    for copy in [given, kept, *row_stores]:
+        copy.wait()
 
 
 def body(diag_blocks, coupling, offsets, arrow_blocks, arrow_index, tip):
@@ -475,20 +559,20 @@
     blocks = jax.ShapeDtypeStruct((count, BS, BS), F32)
     band = 2 * REACH + count
     dma = pltpu.SemaphoreType.DMA
-    lower, handed, schur_tip = pl.pallas_call(
+    u, handed, total = pl.pallas_call(
         kernel,
-        out_shape=(blocks, blocks, jax.ShapeDtypeStruct(tip.shape, F32)),
-        in_specs=[hbm, hbm, smem, hbm, smem, hbm],
-        out_specs=(vmem, vmem, vmem),
+        out_shape=(blocks, blocks, jax.ShapeDtypeStruct((2 * HALF, 8, BS), F32)),
+        in_specs=[hbm, hbm, smem, hbm, smem],
+        out_specs=(vmem, vmem, hbm),
         scratch_shapes=[
             pltpu.VMEM((count, BS, BS), F32),
             pltpu.VMEM((count * width, BS, BS), F32),
             pltpu.VMEM((count, spokes, BS, BS), F32),
-            pltpu.VMEM(tip.shape, F32),
             pltpu.VMEM((count, BS, BS), F32),
             pltpu.VMEM((count, BS, BS), F32),
-            pltpu.VMEM((count, BS, BS), F32),
-            pltpu.VMEM((band, BS, BS), F32),
+            pltpu.VMEM((band // 2, PANEL, BS), F32),
+            pltpu.VMEM((band, PANEL, BS), F32),
+            pltpu.VMEM((band, PANEL, BS), F32),
             pltpu.VMEM((band, BS, 3 * BS), BF16),
             pltpu.VMEM((count * width, 3 * BS, BS), BF16),
             pltpu.VMEM((count, 3 * BS, spokes * BS), BF16),
@@ -503,18 +587,37 @@
             pltpu.VMEM((room, 8, BS), F32),
             pltpu.VMEM((SIZES["y"], 1, 8, BS), F32),
             pltpu.VMEM((2 * HALF, 8, BS), F32),
-            dma((4,)),
-            dma((PANELS, 4)),
-            dma((PANELS, 4)),
-            dma((TOP + 2,)),
-            dma((TOP + 2,)),
+            dma((3,)),
+            dma((2 * len(PARTS),)),
+            dma((len(PIECES), 4)),
+            dma((len(PIECES), 4)),
+            dma((count + PANELS - 1,)),
+            dma((count + PANELS - 1,)),
             dma((copies,)),
             dma((copies,)),
         ],
         compiler_params=pltpu.CompilerParams(
-            collective_id=0, has_side_effects=True, vmem_limit_bytes=56 * 1024 * 1024
+            collective_id=0, has_side_effects=True, vmem_limit_bytes=60 * 1024 * 1024
         ),
-    )(diag_blocks[0], coupling[0].reshape(count * width, BS, BS), offsets[0], arrow_blocks[0], arrow_index[0], tip)
+    )(diag_blocks[0], coupling[0].reshape(count * width, BS, BS), offsets[0], arrow_blocks[0], arrow_index[0])
+    lower, handed, schur_tip = pl.pallas_call(
+        finish_kernel,
+        out_shape=(blocks, blocks, jax.ShapeDtypeStruct(tip.shape, F32)),
+        in_specs=[hbm] * 4,
+        out_specs=(hbm,) * 3,
+        scratch_shapes=[
+            pltpu.VMEM(blocks.shape, F32),
+            pltpu.VMEM(blocks.shape, F32),
+            pltpu.VMEM(total.shape, F32),
+            pltpu.VMEM(tip.shape, F32),
+            pltpu.VMEM(blocks.shape, F32),
+            pltpu.VMEM(tip.shape, F32),
+            dma((6,)),
+            dma((MB,)),
+            dma((MB,)),
+        ],
+        compiler_params=pltpu.CompilerParams(vmem_limit_bytes=60 * 1024 * 1024),
+    )(u, handed, total, tip)
     return (lower[None], handed[None], schur_tip)
 
 

time: 125 us -> 115 us (0.920)
  local copies, waits for them, and re-layouts: 8.13 us -> 0 us
  Pallas kernels: 116 us -> 114 us
    unnamed x3 -> x0, local copies, waits for them, and re-layouts: 8.13 us -> none
    pallas_call x1 -> x2, Pallas kernels: 116 us -> 114 us  [the longest x1 109 us: body(): pl.pallas_call(kernel, out_shape=(blocks, blocks, jax.ShapeDtypeStruct((2...]
where the time goes in v3:
time: 115 us
  Pallas kernels  114 us (99%)
    pallas_call x1, Pallas kernels, body(): pl.pallas_call(kernel, out_shape=(blocks, blocks, jax.ShapeDtypeStruct((2...  109 us
    pallas_call x1, Pallas kernels, body(): pl.pallas_call(finish_kernel, out_shape=(blocks, blocks, jax.ShapeDtypeSt...  5.42 us

profile of v3, /device:TPU:1, one launch (start us, length us, event | category | flops | bytes accessed | tf_op | source)
XLA Modules:
  0.0 115.1 jit_solution(14765749230340386942)
XLA Ops:
  0.6 108.9 %shard_map.85 = (f32[4,128,128]{2,1,0:T(8,128)}, f32[4,128,128]{2,1,0:T(8,128)}, f32[576,8,128]{2,1,0:T(8,128)}) custom-call(f32[4,128,128]{2,1,0:T(8,128)} %bitcast.9, f32[32,128,128]{2,1,0:T(8,128)} %bitcast.7, s32[4,8]{1,0:T(4,128)} %bitcast.10, f32[4,4,128,128]{3,2,1,0:T(8,128)} %bitcast.8, s32[4,4]{1,0:T(4,128)} %bitcast.11), custom_call_target="tpu_custom_call" | custom-call | tf_op jit(solution)/shard_map/pallas_call | solution.py:562
  109.5 5.4 %shard_map.86 = (f32[4,128,128]{2,1,0:T(8,128)}, f32[4,128,128]{2,1,0:T(8,128)}, f32[1024,1024]{1,0:T(8,128)}) custom-call(f32[4,128,128]{2,1,0:T(8,128)} %get-tuple-element.9.u_hbm, f32[4,128,128]{2,1,0:T(8,128)} %get-tuple-element.10.handed_hbm, f32[576,8,128]{2,1,0:T(8,128)} %get-tuple-element.11.res_hbm, f32[1024,1024]{1,0:T(8,128)} %tip_hbm.1), custom_call_target="tpu_custom_call" | custom-call | tf_op jit(solution)/shard_map/pallas_call | solution.py:603

commit v4 on v3

--- a/solution.py
+++ b/solution.py
@@ -20,7 +20,9 @@
 HALF_TILES = 18
 HALF = HALF_TILES * 16
 PARTS = ((0, 128, "xyz"), (128, 128, "yxz"), (256, 32, "zx"))
-PIECES = ((64, 0, 2, 0, 32), (80, 1, 4, 0, 16), (96, 1, 4, 16, 32), (112, 2, 4, 0, 16), (128, 2, 4, 16, 32))
+PIECES = (
+    (64, "pair", 2, 0, 32), (80, "top", 4, 0, 16), (96, "top", 4, 16, 32), (112, "all", 4, 0, 16), (128, "all", 4, 16, 32)
+)
 RELAYED = 3
 
 
@@ -96,7 +98,7 @@
 def kernel(
     diag_hbm, coup_hbm, off_ref, arrow_hbm, idx_ref,
     ubuf, handed_ref, res_hbm,
-    dbuf, cbuf, bbuf, corr, landed, halves, thirds, fourths, wide, cwide, bwide, stacked, early, placed, hi, lo,
+    dbuf, cbuf, bbuf, corr, landed, pieces, wide, cwide, bwide, stacked, placed, hi, lo,
     g_ref, other, acc, bufs, ring, res,
     load_sem, store_sem, win_send, win_recv, dep_send, dep_recv, sum_send, sum_recv,
 ):
@@ -127,8 +129,7 @@
         pltpu.make_async_copy(src, dst, load_sem.at[at])
         for at, (src, dst) in enumerate(((diag_hbm, dbuf), (coup_hbm, cbuf), (arrow_hbm, bbuf)))
     ]
-    for load in loads:
-        load.start()
+    loads[0].start()
 
     barrier = pltpu.get_barrier_semaphore()
     peers = [twin, lat_at(-2), lat_at(2), lat_at(2 * c - 1)]
@@ -140,7 +141,9 @@
     def prepare():
         def couple(at, _):
             ch, cl = split2(cbuf[at])
-            cwide[at] = jnp.concatenate([ch, ch, cl], 0)
+            cwide[at] = jnp.concatenate(
+                [jnp.concatenate([ch, cl], 1), jnp.concatenate([ch, jnp.zeros_like(ch)], 1)], 0
+            )
             return 0
 
         def spoke(n, _):
@@ -170,16 +173,16 @@
         landed[...] = jnp.zeros_like(landed)
 
     loads[0].wait()
+    loads[1].start()
+    loads[2].start()
 
     @pl.when(d > 0)
     def _():
         prepare()
 
-    arrived = (halves, thirds, fourths)
-
     def place_of(step, p):
-        _, buffer, blocks, first, last = PIECES[p]
-        return arrived[buffer].at[pl.ds(step * blocks, blocks), pl.ds(first, last - first)]
+        blocks = PIECES[p][2]
+        return pieces[p].at[pl.ds(step * blocks, blocks)]
 
     def received(p, at, step):
         return remote(place_of(2, p), place_of(step, p), win_send.at[p, at], win_recv.at[p, at], twin)
@@ -213,42 +216,43 @@
         crossing(p).wait_recv()
 
     def pack(p):
-        end, buffer, blocks, first, last = PIECES[p]
+        end, kind, blocks, first, last = PIECES[p]
         rows = end - (last - first)
         value = ubuf[:, rows:end, :]
         lane = lax.broadcasted_iota(jnp.int32, value.shape, 2)
         value = jnp.where(lane <= rows + lax.broadcasted_iota(jnp.int32, value.shape, 1), value, 0.0)
-        if buffer == 0:
+        if kind == "pair":
             half = lane[:2] < BS // 2
             value = jnp.where(half, value[:2], pltpu.roll(value[2:], BS // 2, 2))
-        elif buffer == 1:
+        elif kind == "top":
             top = ubuf[:, first:last, :]
             top = jnp.where(lane <= first + lax.broadcasted_iota(jnp.int32, top.shape, 1), top, 0.0)
             value = jnp.where(lane < BS - PANEL, value, pltpu.roll(top, BS - PANEL, 2))
-        arrived[buffer][2 * blocks : 3 * blocks, first:last, :] = value
+        pieces[p][2 * blocks : 3 * blocks] = value
 
     def widen(rows, blocks, value):
         high, low = split2(value)
-        wide[blocks, rows, :] = jnp.concatenate([high, low, high], 2)
-
-    def unpack(buffers):
+        wide[blocks, rows, :] = jnp.concatenate([high, low], 2)
+
+    def unpack(which):
         for step in range(5):
             inside = (l + step >= 2) & (l + step < lats + 2)
             at = step * count
-            for buffer in buffers:
-                blocks = 2 if buffer == 0 else count
-                value = jnp.where(inside, arrived[buffer][step * blocks : (step + 1) * blocks], 0.0)
+            for p in which:
+                end, kind, blocks, first, last = PIECES[p]
+                rows = slice(end - (last - first), end)
+                value = jnp.where(inside, pieces[p][step * blocks : (step + 1) * blocks], 0.0)
                 lane = lax.broadcasted_iota(jnp.int32, value.shape, 2)
-                if buffer == 0:
+                if kind == "pair":
                     half = lane < BS // 2
-                    widen(slice(32, 64), slice(at, at + 2), jnp.where(half, value, 0.0))
-                    widen(slice(32, 64), slice(at + 2, at + 4), jnp.where(half, pltpu.roll(value, BS // 2, 2), 0.0))
-                elif buffer == 1:
-                    widen(slice(64, 96), slice(at, at + count), jnp.where(lane < BS - PANEL, value, 0.0))
+                    widen(rows, slice(at, at + 2), jnp.where(half, value, 0.0))
+                    widen(rows, slice(at + 2, at + 4), jnp.where(half, pltpu.roll(value, BS // 2, 2), 0.0))
+                elif kind == "top":
+                    widen(rows, slice(at, at + count), jnp.where(lane < BS - PANEL, value, 0.0))
                     top = jnp.where(lane < PANEL, pltpu.roll(value, PANEL, 2), 0.0)
-                    widen(slice(0, 32), slice(at, at + count), top)
+                    widen(slice(first, last), slice(at, at + count), top)
                 else:
-                    widen(slice(96, 128), slice(at, at + count), value)
+                    widen(rows, slice(at, at + count), value)
 
     for p in range(PANELS):
         j0, end = p * PANEL, (p + 1) * PANEL
@@ -293,46 +297,39 @@
                     full = full + jnp.where((ln >= j0) & (ln < end), 0.0, old)
                 corr[m, end:, :] = full
 
-    def update(ranges, hand_on):
+    def update(hand_on):
         for p in range(1, RELAYED):
             hand_over(p)
-        for stage, (first, last) in enumerate(ranges):
-            rows = last - first
-            if first == 0:
-                for p in range(RELAYED):
-                    wait_piece(p)
-                unpack((0, 1))
-            if last == BS:
-                for p in range(RELAYED, len(PIECES)):
-                    hand_over(p)
-                    wait_piece(p)
-                unpack((2,))
-            for m in range(count):
-                for w in range(width):
-                    x = dot(wide[off_ref[m, w] + (m + REACH), first:last, :], cwide[m * width + w])
-                    xh, xl = split2(x)
-                    stacked[w * rows : (w + 1) * rows, :] = jnp.concatenate([xh, xl], 1)
-                both = dot_t(stacked[: width * rows, :BS], stacked[: width * rows, :])
-                if stage:
-                    both = both + early[m]
-                if stage + 1 < len(ranges):
-                    early[m] = both
-                else:
-                    cross = both[:, BS:]
-                    handed_ref[m] = -(both[:, :BS] + cross + cross.T)
-                    if hand_on:
-                        handed_copy(m).start()
+
+        @pl.when(d == 0)
+        def _():
+            prepare()
+
+        for p in range(RELAYED):
+            wait_piece(p)
+        unpack(range(RELAYED))
+        for p in range(RELAYED, len(PIECES)):
+            hand_over(p)
+            wait_piece(p)
+        unpack(range(RELAYED, len(PIECES)))
+        for m in range(count):
+            for w in range(width):
+                x = dot(wide[off_ref[m, w] + (m + REACH)], cwide[m * width + w])
+                xh, xl = split2(x[:, :BS] + x[:, BS:])
+                stacked[m, w * BS : (w + 1) * BS, :] = jnp.concatenate([xh, xl], 1)
+        for m in range(count):
+            both = dot_t(stacked[m, :, :BS], stacked[m])
+            cross = both[:, BS:]
+            handed_ref[m] = -(both[:, :BS] + cross + cross.T)
+            if hand_on:
+                handed_copy(m).start()
         if hand_on:
             for p in range(1, PANELS):
                 handed_copy(count + p - 1).start()
 
-    @pl.when(d == 0)
-    def _():
-        prepare()
-
     @pl.when(d < depths - 1)
     def _():
-        update(((0, 96), (96, 128)), True)
+        update(True)
 
     row = lax.broadcasted_iota(jnp.int32, (BS, BS), 0)
     col = lax.broadcasted_iota(jnp.int32, (BS, BS), 1)
@@ -419,7 +416,7 @@
 
     @pl.when(d == depths - 1)
     def _():
-        update(((0, BS),), False)
+        update(False)
 
     for phase in range(3):
         for part in state:
@@ -570,14 +567,11 @@
             pltpu.VMEM((count, spokes, BS, BS), F32),
             pltpu.VMEM((count, BS, BS), F32),
             pltpu.VMEM((count, BS, BS), F32),
-            pltpu.VMEM((band // 2, PANEL, BS), F32),
-            pltpu.VMEM((band, PANEL, BS), F32),
-            pltpu.VMEM((band, PANEL, BS), F32),
-            pltpu.VMEM((band, BS, 3 * BS), BF16),
-            pltpu.VMEM((count * width, 3 * BS, BS), BF16),
+            tuple(pltpu.VMEM((5 * blocks, last - first, BS), F32) for _, _, blocks, first, last in PIECES),
+            pltpu.VMEM((band, BS, 2 * BS), BF16),
+            pltpu.VMEM((count * width, 2 * BS, 2 * BS), BF16),
             pltpu.VMEM((count, 3 * BS, spokes * BS), BF16),
-            pltpu.VMEM((width * BS, 2 * BS), BF16),
-            pltpu.VMEM((count, BS, 2 * BS), F32),
+            pltpu.VMEM((count, width * BS, 2 * BS), BF16),
             pltpu.VMEM((count, spokes + 1, 2, BS, BS), BF16),
             pltpu.VMEM((count * BS, 12 * BS), BF16),
             pltpu.VMEM((count * BS, 12 * BS), BF16),

time: 115 us -> 114 us (level)
    pallas_call x1, Pallas kernels: 109 us -> 108 us  [body(): pl.pallas_call(kernel, out_shape=(blocks, blocks, jax.ShapeDtypeStruct((2...]
where the time goes in v4:
time: 114 us
  Pallas kernels  113 us (99%)
    pallas_call x1, Pallas kernels, body(): pl.pallas_call(kernel, out_shape=(blocks, blocks, jax.ShapeDtypeStruct((2...  108 us
    pallas_call x1, Pallas kernels, body(): pl.pallas_call(finish_kernel, out_shape=(blocks, blocks, jax.ShapeDtypeSt...  5.42 us

profile of v4, /device:TPU:1, one launch (start us, length us, event | category | flops | bytes accessed | tf_op | source)
XLA Modules:
  0.0 113.7 jit_solution(4328790611637605198)
XLA Ops:
  0.6 107.6 %shard_map.85 = (f32[4,128,128]{2,1,0:T(8,128)}, f32[4,128,128]{2,1,0:T(8,128)}, f32[576,8,128]{2,1,0:T(8,128)}) custom-call(f32[4,128,128]{2,1,0:T(8,128)} %bitcast.9, f32[32,128,128]{2,1,0:T(8,128)} %bitcast.7, s32[4,8]{1,0:T(4,128)} %bitcast.10, f32[4,4,128,128]{3,2,1,0:T(8,128)} %bitcast.8, s32[4,4]{1,0:T(4,128)} %bitcast.11), custom_call_target="tpu_custom_call" | custom-call | tf_op jit(solution)/shard_map/pallas_call | solution.py:559
  108.3 5.4 %shard_map.86 = (f32[4,128,128]{2,1,0:T(8,128)}, f32[4,128,128]{2,1,0:T(8,128)}, f32[1024,1024]{1,0:T(8,128)}) custom-call(f32[4,128,128]{2,1,0:T(8,128)} %get-tuple-element.9.u_hbm, f32[4,128,128]{2,1,0:T(8,128)} %get-tuple-element.10.handed_hbm, f32[576,8,128]{2,1,0:T(8,128)} %get-tuple-element.11.res_hbm, f32[1024,1024]{1,0:T(8,128)} %tip_hbm.1), custom_call_target="tpu_custom_call" | custom-call | tf_op jit(solution)/shard_map/pallas_call | solution.py:597

commit v5 on v4

--- a/solution.py
+++ b/solution.py
@@ -23,7 +23,7 @@
 PIECES = (
     (64, "pair", 2, 0, 32), (80, "top", 4, 0, 16), (96, "top", 4, 16, 32), (112, "all", 4, 0, 16), (128, "all", 4, 16, 32)
 )
-RELAYED = 3
+RELAYED = 4
 
 
 def split2(x):
@@ -97,10 +97,10 @@
 
 def kernel(
     diag_hbm, coup_hbm, off_ref, arrow_hbm, idx_ref,
-    ubuf, handed_ref, res_hbm,
-    dbuf, cbuf, bbuf, corr, landed, pieces, wide, cwide, bwide, stacked, placed, hi, lo,
+    u_hbm, handed_hbm, res_hbm,
+    ubuf, handed_ref, dbuf, cbuf, bbuf, corr, landed, pieces, wide, cwide, bwide, stacked, placed, hi, lo,
     g_ref, other, acc, bufs, ring, res,
-    load_sem, store_sem, win_send, win_recv, dep_send, dep_recv, sum_send, sum_recv,
+    load_sem, store_sem, keep_sem, win_send, win_recv, dep_send, dep_recv, sum_send, sum_recv,
 ):
     depths, lats = lax.axis_size("depth"), lax.axis_size("lat")
     d, l = lax.axis_index("depth"), lax.axis_index("lat")
@@ -130,6 +130,9 @@
         for at, (src, dst) in enumerate(((diag_hbm, dbuf), (coup_hbm, cbuf), (arrow_hbm, bbuf)))
     ]
     loads[0].start()
+
+    keep_u = pltpu.make_async_copy(ubuf, u_hbm, keep_sem.at[0])
+    keep_handed = pltpu.make_async_copy(handed_ref, handed_hbm, keep_sem.at[1])
 
     barrier = pltpu.get_barrier_semaphore()
     peers = [twin, lat_at(-2), lat_at(2), lat_at(2 * c - 1)]
@@ -282,7 +285,7 @@
                         pl.semaphore_wait(barrier, len(peers))
                     for copy in piece_copies(at):
                         copy.start()
-            if row + 16 == PIECES[3][0]:
+            if row + 16 == 112:
                 hand_over(0)
 
         eliminate(part, j0, done)
@@ -326,6 +329,9 @@
         if hand_on:
             for p in range(1, PANELS):
                 handed_copy(count + p - 1).start()
+        keep_handed.start()
+
+    keep_u.start()
 
     @pl.when(d < depths - 1)
     def _():
@@ -353,7 +359,9 @@
     def tile_product(i, first, tiles):
         left = pl.ds(pl.multiple_of(i * BS, BS), BS)
         right = pl.ds(pl.multiple_of(first * BS, BS), tiles * BS)
-        return dot_t(hi[:, left], hi[:, right]) + dot_t(hi[:, left], lo[:, right]) + dot_t(lo[:, left], hi[:, right])
+        high, n = hi[:, right], tiles * BS
+        both = dot_t(hi[:, left], jnp.concatenate([high, lo[:, right]], 1))
+        return both[:, :n] + both[:, n:] + dot_t(lo[:, left], high)
 
     def put(h, k, value):
         g_ref[pl.ds((h * HALF_TILES + k) * 16, 16)] = value.reshape(16, 8, BS)
@@ -476,7 +484,7 @@
         copy.wait_recv()
         stores.append(store(len(stores), theirs, base, n))
 
-    for copy in stores:
+    for copy in [keep_u, keep_handed, *stores]:
         copy.wait()
     for copy in started:
         copy.wait_send()
@@ -552,7 +560,7 @@
             n //= SIZES[axis]
             room += (SIZES[axis] - 1) * n
             copies += 2 * (SIZES[axis] - 1)
-    vmem, smem, hbm = (pl.BlockSpec(memory_space=space) for space in (pltpu.VMEM, pltpu.SMEM, pl.ANY))
+    smem, hbm = (pl.BlockSpec(memory_space=space) for space in (pltpu.SMEM, pl.ANY))
     blocks = jax.ShapeDtypeStruct((count, BS, BS), F32)
     band = 2 * REACH + count
     dma = pltpu.SemaphoreType.DMA
@@ -560,8 +568,10 @@
         kernel,
         out_shape=(blocks, blocks, jax.ShapeDtypeStruct((2 * HALF, 8, BS), F32)),
         in_specs=[hbm, hbm, smem, hbm, smem],
-        out_specs=(vmem, vmem, hbm),
+        out_specs=(hbm, hbm, hbm),
         scratch_shapes=[
+            pltpu.VMEM((count, BS, BS), F32),
+            pltpu.VMEM((count, BS, BS), F32),
             pltpu.VMEM((count, BS, BS), F32),
             pltpu.VMEM((count * width, BS, BS), F32),
             pltpu.VMEM((count, spokes, BS, BS), F32),
@@ -583,6 +593,7 @@
             pltpu.VMEM((2 * HALF, 8, BS), F32),
             dma((3,)),
             dma((2 * len(PARTS),)),
+            dma((2,)),
             dma((len(PIECES), 4)),
             dma((len(PIECES), 4)),
             dma((count + PANELS - 1,)),

time: 114 us -> 113 us (level)
  no operation moved by 1% of the time
where the time goes in v5:
time: 113 us
  Pallas kernels  112 us (99%)
    pallas_call x1, Pallas kernels, body(): pl.pallas_call(kernel, out_shape=(blocks, blocks, jax.ShapeDtypeStruct((2...  107 us
    pallas_call x1, Pallas kernels, body(): pl.pallas_call(finish_kernel, out_shape=(blocks, blocks, jax.ShapeDtypeSt...  5.42 us

profile of v5, /device:TPU:1, one launch (start us, length us, event | category | flops | bytes accessed | tf_op | source)
XLA Modules:
  0.0 112.8 jit_solution(2290840371820736598)
XLA Ops:
  0.6 106.7 %shard_map.85 = (f32[4,128,128]{2,1,0:T(8,128)}, f32[4,128,128]{2,1,0:T(8,128)}, f32[576,8,128]{2,1,0:T(8,128)}) custom-call(f32[4,128,128]{2,1,0:T(8,128)} %bitcast.9, f32[32,128,128]{2,1,0:T(8,128)} %bitcast.7, s32[4,8]{1,0:T(4,128)} %bitcast.10, f32[4,4,128,128]{3,2,1,0:T(8,128)} %bitcast.8, s32[4,4]{1,0:T(4,128)} %bitcast.11), custom_call_target="tpu_custom_call" | custom-call | tf_op jit(solution)/shard_map/pallas_call | solution.py:567
  107.4 5.4 %shard_map.86 = (f32[4,128,128]{2,1,0:T(8,128)}, f32[4,128,128]{2,1,0:T(8,128)}, f32[1024,1024]{1,0:T(8,128)}) custom-call(f32[4,128,128]{2,1,0:T(8,128)} %get-tuple-element.9.u_hbm, f32[4,128,128]{2,1,0:T(8,128)} %get-tuple-element.10.handed_hbm, f32[576,8,128]{2,1,0:T(8,128)} %get-tuple-element.11.res_hbm, f32[1024,1024]{1,0:T(8,128)} %tip_hbm.1), custom_call_target="tpu_custom_call" | custom-call | tf_op jit(solution)/shard_map/pallas_call | solution.py:608

commit v6 on v5

--- a/solution.py
+++ b/solution.py
@@ -24,6 +24,7 @@
     (64, "pair", 2, 0, 32), (80, "top", 4, 0, 16), (96, "top", 4, 16, 32), (112, "all", 4, 0, 16), (128, "all", 4, 16, 32)
 )
 RELAYED = 4
+EARLY = 3
 
 
 def split2(x):
@@ -141,7 +142,7 @@
     for peer in peers:
         pl.semaphore_signal(barrier, inc=1, device_id=peer, device_id_type=MESH)
 
-    def prepare():
+    def split_coupling():
         def couple(at, _):
             ch, cl = split2(cbuf[at])
             cwide[at] = jnp.concatenate(
@@ -149,6 +150,10 @@
             )
             return 0
 
+        loads[1].wait()
+        lax.fori_loop(0, count * width, couple, 0)
+
+    def split_spokes():
         def spoke(n, _):
             for s in range(spokes):
                 bh, bl = split2(bbuf[n, s])
@@ -156,9 +161,7 @@
             placed[n, spokes] = jnp.zeros(placed.shape[2:], BF16)
             return 0
 
-        loads[1].wait()
         loads[2].wait()
-        lax.fori_loop(0, count * width, couple, 0)
         lax.fori_loop(0, count, spoke, 0)
 
     def handed_copy(at):
@@ -181,7 +184,8 @@
 
     @pl.when(d > 0)
     def _():
-        prepare()
+        split_coupling()
+        split_spokes()
 
     def place_of(step, p):
         blocks = PIECES[p][2]
@@ -301,20 +305,23 @@
                 corr[m, end:, :] = full
 
     def update(hand_on):
-        for p in range(1, RELAYED):
+        for p in range(1, EARLY):
             hand_over(p)
 
         @pl.when(d == 0)
         def _():
-            prepare()
-
-        for p in range(RELAYED):
+            split_coupling()
+
+        for p in range(EARLY, RELAYED):
+            hand_over(p)
+        for p in range(EARLY):
             wait_piece(p)
-        unpack(range(RELAYED))
+        unpack(range(EARLY))
         for p in range(RELAYED, len(PIECES)):
             hand_over(p)
+        for p in range(EARLY, len(PIECES)):
             wait_piece(p)
-        unpack(range(RELAYED, len(PIECES)))
+        unpack(range(EARLY, len(PIECES)))
         for m in range(count):
             for w in range(width):
                 x = dot(wide[off_ref[m, w] + (m + REACH)], cwide[m * width + w])
@@ -336,6 +343,10 @@
     @pl.when(d < depths - 1)
     def _():
         update(True)
+
+    @pl.when(d == 0)
+    def _():
+        split_spokes()
 
     row = lax.broadcasted_iota(jnp.int32, (BS, BS), 0)
     col = lax.broadcasted_iota(jnp.int32, (BS, BS), 1)

time: 113 us -> 113 us (level)
  no operation moved by 1% of the time
where the time goes in v6:
time: 113 us
  Pallas kernels  112 us (99%)
    pallas_call x1, Pallas kernels, body(): pl.pallas_call(kernel, out_shape=(blocks, blocks, jax.ShapeDtypeStruct((2...  107 us
    pallas_call x1, Pallas kernels, body(): pl.pallas_call(finish_kernel, out_shape=(blocks, blocks, jax.ShapeDtypeSt...  5.42 us

profile of v6, /device:TPU:1, one launch (start us, length us, event | category | flops | bytes accessed | tf_op | source)
XLA Modules:
  0.0 113.0 jit_solution(10306297931199863711)
XLA Ops:
  0.6 106.9 %shard_map.85 = (f32[4,128,128]{2,1,0:T(8,128)}, f32[4,128,128]{2,1,0:T(8,128)}, f32[576,8,128]{2,1,0:T(8,128)}) custom-call(f32[4,128,128]{2,1,0:T(8,128)} %bitcast.9, f32[32,128,128]{2,1,0:T(8,128)} %bitcast.7, s32[4,8]{1,0:T(4,128)} %bitcast.10, f32[4,4,128,128]{3,2,1,0:T(8,128)} %bitcast.8, s32[4,4]{1,0:T(4,128)} %bitcast.11), custom_call_target="tpu_custom_call" | custom-call | tf_op jit(solution)/shard_map/pallas_call | solution.py:578
  107.5 5.4 %shard_map.86 = (f32[4,128,128]{2,1,0:T(8,128)}, f32[4,128,128]{2,1,0:T(8,128)}, f32[1024,1024]{1,0:T(8,128)}) custom-call(f32[4,128,128]{2,1,0:T(8,128)} %get-tuple-element.9.u_hbm, f32[4,128,128]{2,1,0:T(8,128)} %get-tuple-element.10.handed_hbm, f32[576,8,128]{2,1,0:T(8,128)} %get-tuple-element.11.res_hbm, f32[1024,1024]{1,0:T(8,128)} %tip_hbm.1), custom_call_target="tpu_custom_call" | custom-call | tf_op jit(solution)/shard_map/pallas_call | solution.py:619
